TPU v7x, 32 devices: a whole 2x2x4 slice. The times are simulated.
32 devices in a mesh: grp: 2 (over core), exp: 4 (over y, x), shd: 4 (over z).
Axes of the slice: x: 2, y: 2, z: 4, core: 2. Of those that a mesh axis runs over, the one named last changes fastest.
Arguments:
- tokens_in: bfloat16 [32, 1024, 768], P(('grp', 'exp', 'shd')), may hold values from -6 to 6
- cotangent: bfloat16 [32, 1024, 768], P(('grp', 'exp', 'shd')), may hold values from -6 to 6
- block_ids: int32 [32, 1024], P(('grp', 'exp', 'shd')), may hold values from 0 to 7, never falling along the last dimension, each value on 1 to 256 neighbouring positions
- expert_ids: int32 [32, 1024, 2], P(('grp', 'exp', 'shd')), may hold values from 0 to 3, all different within a row; in each aligned block of 1024 rows (0 to 1023, 1024 to 2047, ..., all dimensions but the last counted through in order) at most 640 rows name the same one
- scales: float32 [2, 768], P(None, ('exp', 'shd')), may hold values from 0.5 to 1.5
- moment_scales: float32 [2, 768], P(None, ('exp', 'shd')), may hold values from -128 to 128
- square_scales: float32 [2, 768], P(None, ('exp', 'shd')), may hold values from 1736.704 to 6881.28
- attend: float32 [3, 768, 768], P(None, ('exp', 'shd')), may hold values from -0.21875 to 0.21875
- moment_attend: float32 [3, 768, 768], P(None, ('exp', 'shd')), may hold values from -64 to 64
- square_attend: float32 [3, 768, 768], P(None, ('exp', 'shd')), may hold values from 425.984 to 1736.704
- output: float32 [768, 768], P(('exp', 'shd')), may hold values from -1.75 to 1.75
- moment_output: float32 [768, 768], P(('exp', 'shd')), may hold values from -7 to 7
- square_output: float32 [768, 768], P(('exp', 'shd')), may hold values from 6.22592 to 24.90368
- router: float32 [768, 4], P(('exp', 'shd')), may hold values from -0.21875 to 0.21875
- moment_router: float32 [768, 4], P(('exp', 'shd')), may hold values from -320 to 320
- square_router: float32 [768, 4], P(('exp', 'shd')), may hold values from 13337.887 to 52848.23
- widener: float32 [2, 768, 2048], P(None, ('exp', 'shd')), may hold values from -0.21875 to 0.21875
- moment_widener: float32 [2, 768, 2048], P(None, ('exp', 'shd')), may hold values from -64 to 64
- square_widener: float32 [2, 768, 2048], P(None, ('exp', 'shd')), may hold values from 425.984 to 1736.704
- reducer: float32 [2048, 768], P(('exp', 'shd')), may hold values from -0.125 to 0.125
- moment_reducer: float32 [2048, 768], P(('exp', 'shd')), may hold values from -64 to 64
- square_reducer: float32 [2048, 768], P(('exp', 'shd')), may hold values from 425.984 to 1736.704
- experts: float32 [4, 2, 768, 2048], P('exp', None, 'shd'), may hold values from -0.21875 to 0.21875
- moment_experts: float32 [4, 2, 768, 2048], P('exp', None, 'shd'), may hold values from -24 to 24
- square_experts: float32 [4, 2, 768, 2048], P('exp', None, 'shd'), may hold values from 68.8128 to 278.528
- narrower: float32 [4, 2048, 768], P('exp', 'shd'), may hold values from -0.125 to 0.125
- moment_narrower: float32 [4, 2048, 768], P('exp', 'shd'), may hold values from -16 to 16
- square_narrower: float32 [4, 2048, 768], P('exp', 'shd'), may hold values from 39.3216 to 157.2864
Outputs:
- block_out: bfloat16 [32, 1024, 768], P(('grp', 'exp', 'shd'))
- input_grad: float32 [32, 1024, 768], P(('grp', 'exp', 'shd'))
- weight_scales: float32 [2, 768], P(None, ('exp', 'shd'))
- first_scales: float32 [2, 768], P(None, ('exp', 'shd'))
- second_scales: float32 [2, 768], P(None, ('exp', 'shd'))
- weight_attend: float32 [3, 768, 768], P(None, ('exp', 'shd'))
- first_attend: float32 [3, 768, 768], P(None, ('exp', 'shd'))
- second_attend: float32 [3, 768, 768], P(None, ('exp', 'shd'))
- weight_output: float32 [768, 768], P(('exp', 'shd'))
- first_output: float32 [768, 768], P(('exp', 'shd'))
- second_output: float32 [768, 768], P(('exp', 'shd'))
- weight_router: float32 [768, 4], P(('exp', 'shd'))
- first_router: float32 [768, 4], P(('exp', 'shd'))
- second_router: float32 [768, 4], P(('exp', 'shd'))
- weight_widener: float32 [2, 768, 2048], P(None, ('exp', 'shd'))
- first_widener: float32 [2, 768, 2048], P(None, ('exp', 'shd'))
- second_widener: float32 [2, 768, 2048], P(None, ('exp', 'shd'))
- weight_reducer: float32 [2048, 768], P(('exp', 'shd'))
- first_reducer: float32 [2048, 768], P(('exp', 'shd'))
- second_reducer: float32 [2048, 768], P(('exp', 'shd'))
- weight_experts: float32 [4, 2, 768, 2048], P('exp', None, 'shd')
- first_experts: float32 [4, 2, 768, 2048], P('exp', None, 'shd')
- second_experts: float32 [4, 2, 768, 2048], P('exp', None, 'shd')
- weight_narrower: float32 [4, 2048, 768], P('exp', 'shd')
- first_narrower: float32 [4, 2048, 768], P('exp', 'shd')
- second_narrower: float32 [4, 2048, 768], P('exp', 'shd')
Inputs may be any that keep to these rules, and one draw needn't show every extreme that they name: `expert_ids`: each token names 2 different experts; of the 1024 tokens of one sequence no expert is named by more than 640, a bound that some block reaches. `block_ids`: never falls along a sequence; each block holds 1 to 256 tokens.
All inputs are finite; a program needn't handle non-finite values.
Results may differ from a plain program's by a relative error of at most 0.014.
The roundings to bfloat16 on the way count: a program that leaves them out, or rounds other values in their place, can miss the bound.
Values may be sent and summed in bfloat16 or wider, within the bound.
A program may use at most 768 MiB of HBM per device.

v0:
```python
import functools

import jax
import jax.numpy as jnp
from jax import lax
from jax.experimental import pallas as pl
from jax.experimental.pallas import tpu as pltpu
from jax.sharding import PartitionSpec as P

HEADS = 12
CAP = 576
VMEM_LIMIT = 60 * 1024 * 1024

norm_eps = 1e-06
adam_eps = 1e-08
beta_one = 0.9
beta_two = 0.95
first_fix = 1.0 - 0.9**10
second_fix = 1.0 - 0.95**10
learning_rates = (0.3, 0.02, 0.15, 0.02, 0.02, 0.012, 0.02, 0.012)
decay_rates = (0.0, 0.1, 0.1, 0.1, 0.1, 0.1, 0.1, 0.1)
masked_score = -1e30
bf16 = jnp.bfloat16
f32 = jnp.float32


def mm(a, b):
    return jnp.dot(a, b, preferred_element_type=f32)


def mm_nt(a, b):
    return lax.dot_general(a, b, (((1,), (1,)), ((), ())), preferred_element_type=f32)


def mm_tn(a, b):
    return lax.dot_general(a, b, (((0,), (0,)), ((), ())), preferred_element_type=f32)


def params(semantics=None, **more):
    return pltpu.CompilerParams(
        dimension_semantics=semantics, vmem_limit_bytes=VMEM_LIMIT, **more
    )


def whole_spec(shape, **more):
    zeros = (0,) * len(shape)
    return pl.BlockSpec(shape, lambda *_: zeros, **more)


def once(shape):
    return whole_spec(shape, pipeline_mode=pl.Buffered(1))


MESH = pl.DeviceIdType.MESH
ANY = pl.BlockSpec(memory_space=pl.ANY)


def greet(targets):
    barrier = pltpu.get_barrier_semaphore()
    for target in targets:
        pl.semaphore_signal(barrier, inc=1, device_id=target, device_id_type=MESH)
    pl.semaphore_wait(barrier, len(targets))


def send(src, dst, send_sem, recv_sem, target):
    return pltpu.make_async_remote_copy(
        src_ref=src, dst_ref=dst, send_sem=send_sem, recv_sem=recv_sem,
        device_id=target, device_id_type=MESH,
    )


def pair_sems(count):
    return [pltpu.SemaphoreType.DMA((count,)), pltpu.SemaphoreType.DMA((count,))]


def others(axis, count):
    me = lax.axis_index(axis)
    return [lax.bitwise_xor(me, k) for k in range(count)]


def gather_kernel(
    exps, shds,
    mine_ref, tiny_ref, pack_ref, g_ref, ids_ref,
    full_ref, every_ref, packs_ref, slots_ref, row_ref, col_ref,
    own_sem, z_send, z_recv, p_send, p_recv, c_send, c_recv, k_send, k_recv,
):
    columns, layers = others("exp", exps), others("shd", shds)
    group = lax.axis_index("grp")
    core = lax.rem(group, 2)
    partner = {"grp": lax.bitwise_xor(group, 1)}
    rows = mine_ref.shape[1]
    relay = exps == 4
    direct = range(1, 3 if relay else exps)

    def spots(kz, kx):
        at = pl.ds(pl.multiple_of((columns[kx] * shds + layers[kz]) * rows, 16), rows)
        return full_ref.at[pl.ds(2 * core, 2), at, :], every_ref.at[at, :]

    greet(
        [{"shd": layer} for layer in layers[1:]]
        + [{"exp": column} for column in columns[1:]]
        + [partner]
    )
    started = []

    def begin(copies):
        for copy in copies:
            copy.start()
        started.extend(copies)
        return copies

    def both(sources, kz, kx, sem, far, index, target):
        return [
            send(a, b, sem.at[index + (i,)], far.at[index + (i,)], target)
            for i, (a, b) in enumerate(zip(sources, spots(kz, kx)))
        ]

    mine = (mine_ref, tiny_ref)
    local = [
        pltpu.make_async_copy(a, b, own_sem.at[i])
        for i, (a, b) in enumerate(zip(mine, spots(0, 0)))
    ]
    for copy in local:
        copy.start()
    down = [both(mine, 0, 0, z_send, z_recv, (k,), {"shd": layers[k]}) for k in range(1, shds)]
    for copies in down:
        begin(copies)
    across = {}
    for kx in direct:
        across[0, kx] = begin(both(mine, 0, 0, p_send, p_recv, (0, kx), {"exp": columns[kx]}))
    packs = [pltpu.make_async_copy(pack_ref, packs_ref.at[columns[0]], k_send.at[0])]
    for kx in direct:
        packs.append(
            send(pack_ref, packs_ref.at[columns[0]], k_send.at[kx], k_recv.at[kx], {"exp": columns[kx]})
        )
    for copy in packs:
        copy.start()
    swaps = [send(mine_ref, spots(0, 0)[0], c_send.at[0, 0], c_recv.at[0, 0], partner)]
    swaps[0].start()
    seq = g_ref.shape[0]
    expert = lax.broadcasted_iota(jnp.int32, (16, seq), 0)
    named = (ids_ref[0:1, :] == expert) | (ids_ref[1:2, :] == expert)
    earlier = lax.broadcasted_iota(jnp.int32, (seq, seq), 0) < lax.broadcasted_iota(jnp.int32, (seq, seq), 1)
    count = mm(named.astype(f32).astype(bf16), earlier.astype(f32).astype(bf16))
    place = jnp.where(named, count, -1.0)
    row_ref[...] = place.astype(jnp.int32)
    col_ref[...] = jnp.concatenate([place, jnp.full((112, seq), -1.0, f32)], axis=0).T.astype(jnp.int32)

    def fill(e):
        hot = slots_of(row_ref[e : e + 1, :], slots_ref.shape[1])
        slots_ref[e] = mm(hot, g_ref[...]).astype(bf16)

    def swap(kz, kx):
        here = spots(kz, kx)[0]
        copy = send(here, here, c_send.at[kz, kx], c_recv.at[kz, kx], partner)
        copy.start()
        swaps.append(copy)

    for kz in range(1, shds):
        for copy in down[kz - 1]:
            copy.wait_recv()
        for kx in direct:
            across[kz, kx] = begin(both(spots(kz, 0), kz, 0, p_send, p_recv, (kz, kx), {"exp": columns[kx]}))
        swap(kz, 0)
        if kz <= slots_ref.shape[0]:
            fill(kz - 1)
    for e in range(shds - 1, slots_ref.shape[0]):
        fill(e)
    if relay:
        half = pack_ref.shape[0] // 2
        for kx in direct:
            packs[kx].wait_recv()
            spot = packs_ref.at[columns[kx], pl.ds(half * (kx - 1), half), :]
            copy = send(spot, spot, k_send.at[2 + kx], k_recv.at[2 + kx], {"exp": columns[3 - kx]})
            copy.start()
            packs.append(copy)
    for kz in range(shds):
        via = 1 + kz % 2
        for kx in direct:
            for copy in across[kz, kx]:
                copy.wait_recv()
            if relay and kx == via:
                across[kz, 3] = begin(
                    both(spots(kz, kx), kz, kx, p_send, p_recv, (kz, 3), {"exp": columns[3 - via]})
                )
            swap(kz, kx)
    if relay:
        for kz in range(shds):
            for copy in across[kz, 3]:
                copy.wait_recv()
            swap(kz, 3)
    for copy in started:
        copy.wait_send()
    if relay:
        for kx in direct:
            packs[kx].wait_send()
        packs = packs[:1] + packs[3:]
    for copy in swaps + local + packs:
        copy.wait()


def gather_first(mine, tiny, pack, g, ids, exps, shds, experts_all, cap):
    _, rows, width = mine.shape
    tall = exps * shds * rows
    sems = lambda *shape: pltpu.SemaphoreType.DMA(shape)
    return pl.pallas_call(
        functools.partial(gather_kernel, exps, shds),
        in_specs=[ANY, ANY, ANY] + [pl.BlockSpec(memory_space=pltpu.VMEM)] * 2,
        out_specs=[ANY, ANY, ANY] + [pl.BlockSpec(memory_space=pltpu.VMEM)] * 3,
        out_shape=[
            jax.ShapeDtypeStruct((4, tall, width), bf16),
            jax.ShapeDtypeStruct((tall, 128), bf16),
            jax.ShapeDtypeStruct((exps,) + pack.shape, bf16),
            jax.ShapeDtypeStruct((experts_all, cap, width), bf16),
            jax.ShapeDtypeStruct((16, g.shape[0]), jnp.int32),
            jax.ShapeDtypeStruct((g.shape[0], 128), jnp.int32),
        ],
        scratch_shapes=[
            sems(2), sems(shds, 2), sems(shds, 2), sems(shds, exps, 2), sems(shds, exps, 2),
            sems(shds, exps), sems(shds, exps), sems(exps + 1), sems(exps + 1),
        ],
        compiler_params=params(collective_id=4, has_side_effects=True),
        cost_estimate=pl.CostEstimate(
            flops=40_000_000_000, bytes_accessed=10_000_000, transcendentals=0
        ),
        name="gather_first",
    )(mine, tiny, pack, g, ids)


def forward_kernel(
    exps,
    tok_ref, bidr_ref, bidc_ref, wa_ref, wo_ref, wr_ref, slots_ref,
    qkv_ref, lse_ref, o_ref, mid_ref, h2_ref, probs_ref, probst_ref, gains_ref, landed_ref, h1_ref,
    send_sem, recv_sem,
):
    pair = pl.program_id(0)
    me = lax.axis_index("exp")

    def copies():
        made = [pltpu.make_async_copy(slots_ref.at[me], landed_ref.at[0], send_sem.at[0])]
        for k in range(1, exps):
            peer = lax.bitwise_xor(me, k)
            made.append(
                send(slots_ref.at[peer], landed_ref.at[k], send_sem.at[k], recv_sem.at[k], {"exp": peer})
            )
        return made

    @pl.when(pair == 0)
    def _():
        greet([{"exp": lax.bitwise_xor(me, k)} for k in range(1, exps)])
        for copy in copies():
            copy.start()
    seq, width = tok_ref.shape
    tile = 256

    @pl.when(pair == 0)
    def _():
        gains_ref[...] = wr_ref[...].astype(f32).T[:8]
        for row in range(0, seq, tile):
            x = tok_ref[pl.ds(row, tile), :].astype(f32)
            r1 = lax.rsqrt(jnp.mean(x * x, axis=1, keepdims=True) + norm_eps)
            h1_ref[pl.ds(row, tile), :] = (x * r1 * gains_ref[4:5, :]).astype(bf16)

    h1 = h1_ref[...]
    for i in range(3):
        qkv_ref[i] = mm(h1, wa_ref[i]).astype(bf16)
    qs = qkv_ref[0] * jnp.asarray(0.125, bf16)
    k = qkv_ref[1]
    vt = qkv_ref[2].T
    lane = lax.broadcasted_iota(jnp.int32, (tile, 128), 1)
    for q0 in range(0, seq, tile):
        kl = min(seq, q0 + 2 * tile)
        qt = qs[q0 : q0 + tile]
        allowed = bidc_ref[q0:kl, :] <= bidr_ref[0:1, q0 : q0 + tile]
        parts = []
        for head in range(2):
            qm = jnp.where((lane // 64) == head, qt, jnp.zeros_like(qt))
            tail = jnp.where(allowed, mm_nt(k[q0:kl], qm), masked_score)
            top = jnp.max(tail, axis=0, keepdims=True)
            if q0:
                lead = mm_nt(k[:q0], qm)
                top = jnp.maximum(top, jnp.max(lead, axis=0, keepdims=True))
                lead = jnp.exp(lead - top)
            tail = jnp.exp(tail - top)
            total = jnp.sum(tail, axis=0, keepdims=True)
            if q0:
                total = total + jnp.sum(lead, axis=0, keepdims=True)
            inverse = 1.0 / total
            vh = vt[64 * head : 64 * head + 64]
            ot = mm(vh[:, q0:kl], (tail * inverse).astype(bf16))
            if q0:
                ot = ot + mm(vh[:, :q0], (lead * inverse).astype(bf16))
            lse_ref[0, head : head + 1, q0 : q0 + tile] = top + jnp.log(total)
            parts.append(ot)
        out = jnp.concatenate(parts, axis=0).T.astype(bf16)
        o_ref[q0 : q0 + tile, pl.ds(pl.multiple_of(pair * 128, 128), 128)] = out

    @pl.when(pair == pl.num_programs(0) - 1)
    def _():
        for row in range(0, seq, tile):
            rows = pl.ds(row, tile)
            mid = tok_ref[rows, :].astype(f32) + mm(o_ref[rows, :], wo_ref[0])
            mid_ref[rows, :] = mid
            r2 = lax.rsqrt(jnp.mean(mid * mid, axis=1, keepdims=True) + norm_eps)
            h2 = (mid * r2 * gains_ref[5:6, :]).astype(bf16)
            h2_ref[rows, :] = h2
            logits = mm(h2, wr_ref[...])
            spot = lax.broadcasted_iota(jnp.int32, logits.shape, 1)
            logits = jnp.where(spot < 4, logits, masked_score)
            e = jnp.exp(logits - jnp.max(logits, axis=1, keepdims=True))
            probs_ref[rows, :] = e / jnp.sum(e, axis=1, keepdims=True)
        routers = gains_ref[...].astype(bf16)
        logits = mm_nt(jnp.concatenate([routers, routers], axis=0), h2_ref[...])
        spot = lax.broadcasted_iota(jnp.int32, logits.shape, 0)
        logits = jnp.where(spot < 4, logits, masked_score)
        e = jnp.exp(logits - jnp.max(logits, axis=0, keepdims=True))
        probst_ref[...] = e / jnp.sum(e, axis=0, keepdims=True)
        for copy in copies():
            copy.wait()


def attention_forward(tokens, bid_row, bid_col, full, wr, slots):
    exps = slots.shape[0]
    seq, width = tokens.shape
    pairs = width // 128
    return pl.pallas_call(
        functools.partial(forward_kernel, exps),
        grid=(pairs,),
        in_specs=[
            once((seq, width)),
            once(bid_row.shape),
            once(bid_col.shape),
            pl.BlockSpec((3, width, 128), lambda i: (0, 0, i)),
            pl.BlockSpec((1, width, width), lambda i: (3, 0, 0), pipeline_mode=pl.Buffered(1)),
            once(wr.shape),
            ANY,
        ],
        out_specs=[
            pl.BlockSpec((3, seq, 128), lambda i: (0, 0, i)),
            pl.BlockSpec((1, 8, seq), lambda i: (i, 0, 0)),
            whole_spec((seq, width)),
            whole_spec((seq, width)),
            whole_spec((seq, width)),
            whole_spec((seq, 128)),
            whole_spec((16, seq)),
            whole_spec((8, width)),
            ANY,
        ],
        out_shape=[
            jax.ShapeDtypeStruct((3, seq, width), bf16),
            jax.ShapeDtypeStruct((pairs, 8, seq), f32),
            jax.ShapeDtypeStruct((seq, width), bf16),
            jax.ShapeDtypeStruct((seq, width), f32),
            jax.ShapeDtypeStruct((seq, width), bf16),
            jax.ShapeDtypeStruct((seq, 128), f32),
            jax.ShapeDtypeStruct((16, seq), f32),
            jax.ShapeDtypeStruct((8, width), f32),
            jax.ShapeDtypeStruct(slots.shape, bf16),
        ],
        scratch_shapes=[pltpu.VMEM((seq, width), bf16)] + pair_sems(exps),
        compiler_params=params(("arbitrary",), collective_id=1, has_side_effects=True),
        cost_estimate=pl.CostEstimate(
            flops=30_000_000_000, bytes_accessed=20_000_000, transcendentals=12_000_000
        ),
        name="attention_forward",
    )(tokens, bid_row, bid_col, full, full, wr, slots)


def slots_of(place_row, cap):
    slot = lax.broadcasted_iota(jnp.int32, (cap, place_row.shape[1]), 0)
    return (slot == place_row).astype(f32).astype(bf16)


def dispatch_kernel(h2_ref, place_ref, probst_ref, rows_ref, chosen_ref):
    expert = pl.program_id(0)
    cap = rows_ref.shape[1]
    lanes = chosen_ref.shape[2]
    row = place_ref[pl.ds(expert, 1), :]
    rows_ref[0] = mm(slots_of(row, cap), h2_ref[...]).astype(bf16)
    value = probst_ref[pl.ds(expert, 1), :]
    high = value.astype(bf16)
    rest = value - high.astype(f32)
    middle = rest.astype(bf16)
    low = (rest - middle.astype(f32)).astype(bf16)
    spot = lax.broadcasted_iota(jnp.int32, (16, row.shape[1]), 0)
    pieces = jnp.where(
        spot == 0, high.astype(f32), jnp.where(spot == 1, middle.astype(f32), jnp.where(spot == 2, low.astype(f32), 0.0))
    )
    chosen = jnp.sum(mm_nt(pieces.astype(bf16), slots_of(row, lanes)), axis=0, keepdims=True)
    chosen_ref[0] = jnp.broadcast_to(chosen, chosen_ref.shape[1:])


def dispatch(h2, place_row, probst, experts_all, cap, lanes):
    seq, width = h2.shape
    return pl.pallas_call(
        dispatch_kernel,
        grid=(experts_all,),
        in_specs=[once(h2.shape), once(place_row.shape), once(probst.shape)],
        out_specs=[
            pl.BlockSpec((1, cap, width), lambda e: (e, 0, 0)),
            pl.BlockSpec((1, 8, lanes), lambda e: (e, 0, 0)),
        ],
        out_shape=[
            jax.ShapeDtypeStruct((experts_all, cap, width), bf16),
            jax.ShapeDtypeStruct((experts_all, 8, lanes), f32),
        ],
        compiler_params=params(("arbitrary",)),
        cost_estimate=pl.CostEstimate(
            flops=5_000_000_000, bytes_accessed=6_000_000, transcendentals=0
        ),
        name="dispatch",
    )(h2, place_row, probst)


def gated(x, g, wg, wu, wn):
    gate, up = mm(x, wg), mm(x, wu)
    hgrad = mm_nt(g, wn)
    sig = lax.logistic(gate)
    active = gate * sig
    slope = sig * (1.0 + gate * (1.0 - sig))
    hidden = (active * up).astype(bf16)
    return hidden, (hgrad * up * slope).astype(bf16), (hgrad * active).astype(bf16)


def routed_kernel(
    exps, shds,
    rows_ref, chosen_ref, grads_ref, packed_ref,
    eout_ref, gin_ref, sum_ref,
    x_s, g_s, c_s, w_s, n_s, hid_s, gg_s, ug_s, out_s, gin_s, wide_l, narrow_l,
    load_sem, x_send, x_recv, c_send, c_recv, o_send, o_recv, i_send, w_sem, s_send, s_recv,
):
    me = lax.axis_index("exp")
    _, cap, width = x_s.shape
    hidden = hid_s.shape[1]
    rows_all = exps * cap
    peers = [lax.bitwise_xor(me, k) for k in range(exps)]
    group = lax.axis_index("grp")
    core = lax.rem(group, 2)
    partner = {"grp": lax.bitwise_xor(group, 1)}
    greet([{"exp": peer} for peer in peers[1:]] + [partner])
    deep, tall = w_s.shape[2], n_s.shape[2]
    base = hidden // 256 * deep
    wide_at = lambda b: pl.ds(pl.multiple_of(b * deep, 16), deep)
    narrow_at = lambda b: pl.ds(base + b * tall, tall)
    lanes_at = lambda b: pl.ds(pl.multiple_of(256 * b, 256), 256)

    chosen, arriving = [], []
    for k in range(1, exps):
        target = {"exp": peers[k]}
        chosen.append(send(chosen_ref.at[peers[k]], c_s.at[k], c_send.at[k], c_recv.at[k], target))
        arriving.append(send(rows_ref.at[peers[k]], x_s.at[k], x_send.at[k], x_recv.at[k], target))
    for copy in chosen + arriving[:2]:
        copy.start()
    loads = [
        pltpu.make_async_copy(rows_ref.at[me], x_s.at[0], load_sem.at[0]),
        pltpu.make_async_copy(chosen_ref.at[me], c_s.at[0], load_sem.at[1]),
        pltpu.make_async_copy(grads_ref, g_s, load_sem.at[2]),
    ]
    for c in range(2):
        for b in range(hidden // 256):
            loads.append(
                pltpu.make_async_copy(
                    packed_ref.at[c, :, wide_at(b), :], w_s.at[c, :, :, lanes_at(b)], load_sem.at[len(loads)]
                )
            )
        for b in range(width // 256):
            loads.append(
                pltpu.make_async_copy(
                    packed_ref.at[c, :, narrow_at(b), :], n_s.at[:, c, :, lanes_at(b)], load_sem.at[len(loads)]
                )
            )
    for copy in loads:
        copy.start()
    for copy in loads:
        copy.wait()

    ft = 512
    returns, kept = [], []
    for k in range(exps):
        if k:
            chosen[k - 1].wait()
            arriving[k - 1].wait()
        scale = c_s[k].T[:cap, 0:1]
        g_s[k] = (g_s[k].astype(f32) * scale).astype(bf16)

        @pl.loop(0, hidden // ft)
        def _(f):
            columns = pl.ds(pl.multiple_of(f * ft, ft), ft)
            wg = w_s[0, :, :, columns].reshape(width, ft)
            wu = w_s[1, :, :, columns].reshape(width, ft)
            hid, gg, ug = gated(x_s[k], g_s[k], wg, wu, n_s[f].reshape(ft, width))
            hid_s[pl.ds(k * cap, cap), columns] = hid
            gg_s[pl.ds(k * cap, cap), columns] = gg
            ug_s[pl.ds(k * cap, cap), columns] = ug

        mine = pl.ds(k * cap, cap)
        if k >= 2:
            kept[k - 2].wait()
        for b in range(width // 256):
            part = slice(256 * b, 256 * b + 256)
            out_s[k, :, part] = mm(hid_s[mine, :], n_s[:, :, :, part].reshape(hidden, 256)).astype(bf16)
            wg = w_s[0].reshape(width, hidden)[part]
            wu = w_s[1].reshape(width, hidden)[part]
            gin_s[k % 2, :, part] = (mm_nt(gg_s[mine, :], wg) + mm_nt(ug_s[mine, :], wu)).astype(bf16)

        if k:
            back = send(
                out_s.at[k], eout_ref.at[me], o_send.at[k], o_recv.at[k], {"exp": peers[k]}
            )
        else:
            back = pltpu.make_async_copy(out_s.at[0], eout_ref.at[me], o_send.at[0])
            for copy in arriving[2:]:
                copy.start()
        kept.append(pltpu.make_async_copy(gin_s.at[k % 2], gin_ref.at[peers[k]], i_send.at[k]))
        for copy in (back, kept[k]):
            copy.start()
        returns.append(back)

    wide = hidden // shds
    per = wide // 256

    across = lambda f: pl.ds(pl.multiple_of(f * wide, wide), wide)

    def swaps(f):
        return [
            send(w_s.at[1 - core, :, :, across(f)], wide_l.at[f], s_send.at[f, 0], s_recv.at[f, 0], partner),
            send(n_s.at[f, 1 - core], narrow_l.at[f], s_send.at[f, 1], s_recv.at[f, 1], partner),
        ]

    def stores(f):
        made = []
        for b in range(per):
            block = per * f + b
            made.append((w_s.at[core, :, :, lanes_at(block)], sum_ref.at[:, wide_at(block), :]))
        for b in range(width // 256):
            made.append((n_s.at[f, core, :, lanes_at(b)], sum_ref.at[f, narrow_at(b), :]))
        return [pltpu.make_async_copy(a, b, w_sem.at[f, i]) for i, (a, b) in enumerate(made)]

    def add(f):
        for copy in swaps(f):
            copy.wait_recv()
        for z in range(shds):
            own = w_s[core, z, :, across(f)].astype(f32)
            w_s[core, z, :, across(f)] = (own + wide_l[f, z].astype(f32)).astype(bf16)
        n_s[f, core] = (n_s[f, core].astype(f32) + narrow_l[f].astype(f32)).astype(bf16)
        for copy in stores(f):
            copy.start()

    @pl.loop(0, shds)
    def _(f):
        columns = pl.ds(pl.multiple_of(f * wide, wide), wide)
        x = x_s[...].reshape(rows_all, width)
        g = g_s[...].reshape(rows_all, width)
        part = w_s.shape[1:3] + (wide,)
        w_s[0, :, :, columns] = mm_tn(x, gg_s[:, columns]).astype(bf16).reshape(part)
        w_s[1, :, :, columns] = mm_tn(x, ug_s[:, columns]).astype(bf16).reshape(part)
        n_s[f] = mm_tn(hid_s[:, columns], g).astype(bf16).reshape(n_s.shape[1:])
        for copy in swaps(f):
            copy.start()

        @pl.when(f > 0)
        def _():
            add(f - 1)

    add(shds - 1)
    for copy in returns + kept[-2:]:
        copy.wait()

    @pl.loop(0, shds)
    def _(f):
        for copy in swaps(f):
            copy.wait_send()
        for copy in stores(f):
            copy.wait()


def routed(slot_rows, chosen, grads, packed, hidden):
    exps, cap, width = slot_rows.shape
    shds, height = packed.shape[1:3]
    deep, tall = width // shds, hidden // shds // 2
    pieces = hidden // shds // 256 + width // 256
    big = lambda *shape: pltpu.VMEM(shape, bf16)
    sems = lambda *n: pltpu.SemaphoreType.DMA(n)
    return pl.pallas_call(
        functools.partial(routed_kernel, exps, shds),
        in_specs=[ANY] * 4,
        out_specs=[ANY] * 3,
        out_shape=[
            jax.ShapeDtypeStruct((exps, cap, width), bf16),
            jax.ShapeDtypeStruct((exps, cap, width), bf16),
            jax.ShapeDtypeStruct((shds, height, 256), bf16),
        ],
        scratch_shapes=[
            big(exps, cap, width),
            big(exps, cap, width),
            pltpu.VMEM(chosen.shape, f32),
            big(2, shds, deep, hidden),
            big(shds, 2, tall, width),
            big(exps * cap, hidden),
            big(exps * cap, hidden),
            big(exps * cap, hidden),
            big(exps, cap, width),
            big(2, cap, width),
            big(shds, shds, deep, hidden // shds),
            big(shds, tall, width),
            sems(3 + 2 * (hidden // 256 + width // 256)),
            sems(exps), sems(exps), sems(exps), sems(exps), sems(exps), sems(exps), sems(exps),
            sems(shds, pieces), sems(shds, 2), sems(shds, 2),
        ],
        compiler_params=params(collective_id=2, has_side_effects=True),
        cost_estimate=pl.CostEstimate(
            flops=18 * exps * cap * width * hidden,
            bytes_accessed=40_000_000,
            transcendentals=exps * cap * hidden,
        ),
        name="routed",
    )(slot_rows, chosen, grads, packed)


def ffn_kernel(
    x_ref, g_ref, wg_ref, wu_ref, wn_ref, back_ref,
    out_ref, gin_ref, part_a, part_b, ein_ref,
    acc_out, acc_gin, hid_s, gg_s, ug_s, wide_s, narrow_s, wide_l, narrow_l,
    own_sem, send_sem, recv_sem, b_send, b_recv,
    *, tile,
):
    f = pl.program_id(0)
    last = pl.num_programs(0) - 1
    rows_all, width = x_ref.shape
    group = lax.axis_index("grp")
    core = lax.rem(group, 2)
    partner = {"grp": lax.bitwise_xor(group, 1)}
    ft = wide_s.shape[3]
    shards, tall = narrow_s.shape[2:4]

    def swaps(step):
        return [
            send(a.at[step, b], c.at[step], send_sem.at[step, i], recv_sem.at[step, i], partner)
            for i, (a, b, c) in enumerate(
                [(wide_s, 1 - core, wide_l), (narrow_s, 1 - core, narrow_l)]
            )
        ]

    def stores(step):
        columns = pl.ds(pl.multiple_of(step * ft, ft), ft)
        at = pl.ds(step * shards, shards)
        return [
            pltpu.make_async_copy(wide_s.at[step, core], part_a.at[:, columns], own_sem.at[step, 0]),
            pltpu.make_async_copy(narrow_s.at[step, core], part_b.at[at], own_sem.at[step, 1]),
        ]

    def add(step):
        for copy in swaps(step):
            copy.wait_recv()
        wide_s[step, core] = (wide_s[step, core].astype(f32) + wide_l[step].astype(f32)).astype(bf16)
        narrow_s[step, core] = (narrow_s[step, core].astype(f32) + narrow_l[step].astype(f32)).astype(bf16)
        for copy in stores(step):
            copy.start()

    exps = back_ref.shape[0]
    columns = others("exp", exps)

    def returns():
        me = columns[0]
        made = [pltpu.make_async_copy(back_ref.at[me], ein_ref.at[me], b_send.at[0])]
        for k in range(1, exps):
            made.append(
                send(
                    back_ref.at[columns[k]], ein_ref.at[me],
                    b_send.at[k], b_recv.at[k], {"exp": columns[k]},
                )
            )
        return made

    @pl.when(f == 0)
    def _():
        greet([{"exp": column} for column in columns[1:]] + [partner])
        for copy in returns():
            copy.start()
        acc_out[...] = jnp.zeros_like(acc_out)
        acc_gin[...] = jnp.zeros_like(acc_gin)

    deep = wg_ref.shape[3] // 2
    order = [(z, e) for e in range(wg_ref.shape[2]) for z in range(wg_ref.shape[1])]

    def wide(ref):
        blocks = [
            jnp.concatenate([ref[0, z, e, deep * b : deep * (b + 1)] for z, e in order], axis=0)
            for b in range(2)
        ]
        return jnp.concatenate(blocks, axis=1)

    wg, wu = wide(wg_ref), wide(wu_ref)
    narrow = [
        jnp.concatenate([wn_ref[c, z, e, tall * b : tall * (b + 1)] for b in range(width // 256)], axis=1)
        for e in range(wn_ref.shape[2])
        for z in range(wn_ref.shape[1])
        for c in range(2)
    ]
    wn = jnp.concatenate(narrow, axis=0)
    for row in range(0, rows_all, tile):
        rows = pl.ds(row, tile)
        x, g = x_ref[rows, :], g_ref[rows, :]
        hidden, gg, ug = gated(x, g, wg, wu, wn)
        hid_s[rows, :], gg_s[rows, :], ug_s[rows, :] = hidden, gg, ug
        acc_out[rows, :] += mm(hidden, wn)
        acc_gin[rows, :] += mm_nt(gg, wg) + mm_nt(ug, wu)
    wide_s[f, 0] = mm_tn(x_ref[...], gg_s[...]).astype(bf16)
    wide_s[f, 1] = mm_tn(x_ref[...], ug_s[...]).astype(bf16)
    narrow = mm_tn(hid_s[...], g_ref[...]).astype(bf16).reshape(shards, 2, tall, width)
    for c in range(2):
        narrow_s[f, c] = narrow[:, c]
    for copy in swaps(f):
        copy.start()

    @pl.when(f > 0)
    def _():
        add(f - 1)

    @pl.when(f == last)
    def _():
        out_ref[...] = acc_out[...].astype(out_ref.dtype)
        gin_ref[...] = acc_gin[...].astype(gin_ref.dtype)

        add(last)

        @pl.loop(0, pl.num_programs(0))
        def _(step):
            for copy in swaps(step):
                copy.wait_send()
            for copy in stores(step):
                copy.wait()

        for copy in returns():
            copy.wait()


def ffn(x, g, packed, back, hidden, out_type, tile, name):
    rows, width = x.shape
    _, shds, exps, height, _ = packed.shape
    spread = shds * exps
    ft = 512
    steps = hidden // ft
    deep, tall = width // spread, hidden // spread // 2
    shards = spread // steps
    base = hidden // 256 * deep
    narrow_high = height - base
    sems = pltpu.SemaphoreType.DMA((steps, 2))
    return pl.pallas_call(
        functools.partial(ffn_kernel, tile=tile),
        grid=(steps,),
        in_specs=[
            once((rows, width)),
            once((rows, width)),
            pl.BlockSpec((1, shds, exps, 2 * deep, 256), lambda f: (0, 0, 0, f, 0)),
            pl.BlockSpec((1, shds, exps, 2 * deep, 256), lambda f: (1, 0, 0, f, 0)),
            pl.BlockSpec((2, shds, shards // shds, narrow_high, 256), lambda f: (0, 0, f, base // narrow_high, 0)),
            ANY,
        ],
        out_specs=[once((rows, width)), once((rows, width)), ANY, ANY, ANY],
        out_shape=[
            jax.ShapeDtypeStruct((rows, width), out_type),
            jax.ShapeDtypeStruct((rows, width), out_type),
            jax.ShapeDtypeStruct((width, hidden), bf16),
            jax.ShapeDtypeStruct((spread, tall, width), bf16),
            jax.ShapeDtypeStruct(back.shape, bf16),
        ],
        scratch_shapes=[
            pltpu.VMEM((rows, width), f32),
            pltpu.VMEM((rows, width), f32),
            pltpu.VMEM((rows, ft), bf16),
            pltpu.VMEM((rows, ft), bf16),
            pltpu.VMEM((rows, ft), bf16),
            pltpu.VMEM((steps, 2, width, ft), bf16),
            pltpu.VMEM((steps, 2, shards, tall, width), bf16),
            pltpu.VMEM((steps, width, ft), bf16),
            pltpu.VMEM((steps, shards, tall, width), bf16),
            sems, sems, sems,
        ]
        + pair_sems(back.shape[0]),
        compiler_params=params(("arbitrary",), collective_id=3, has_side_effects=True),
        cost_estimate=pl.CostEstimate(
            flops=18 * rows * width * hidden,
            bytes_accessed=12 * width * hidden + 8 * rows * width,
            transcendentals=rows * hidden,
        ),
        name=name,
    )(x, g, packed, packed, packed, back)


def plane_copies(exps, block_for, landed_ref, send_sem, recv_sem):
    columns = others("exp", exps)
    made = [pltpu.make_async_copy(block_for(columns[0]), landed_ref.at[0], send_sem.at[0])]
    for k in range(1, exps):
        made.append(
            send(
                block_for(columns[k]), landed_ref.at[k],
                send_sem.at[k], recv_sem.at[k], {"exp": columns[k]},
            )
        )
    return made


def combine_kernel(
    mid_ref, sout_ref, sin_ref, g_ref, h2_ref, probs_ref, place_ref, eout_ref, ein_ref,
    gains_ref, wr_ref, wo_ref, part_ref,
    block_ref, midg_ref, midb_ref, og_ref, gain_ref, rgrad_ref, landed_ref,
    send_sem, recv_sem,
):
    step = pl.program_id(0)
    exps = part_ref.shape[0]
    exchange = lambda: plane_copies(exps, lambda c: part_ref.at[c], landed_ref, send_sem, recv_sem)

    @pl.when(step == 0)
    def _():
        greet([{"exp": column} for column in others("exp", exps)[1:]])
        for copy in exchange():
            copy.start()

    tile, width = mid_ref.shape
    experts_all, cap = eout_ref.shape[0], eout_ref.shape[1]
    slot = lax.broadcasted_iota(jnp.int32, (tile, cap), 1)
    g = g_ref[...].astype(f32)
    probs = probs_ref[...]
    spot = lax.broadcasted_iota(jnp.int32, probs.shape, 1)
    mixture = jnp.zeros((tile, width), f32)
    moe_in = jnp.zeros((tile, width), f32)
    pgrad = jnp.zeros(probs.shape, f32)
    for e in range(experts_all):
        hot = (slot == place_ref[:, e : e + 1]).astype(f32).astype(bf16)
        pair_out = mm(hot, eout_ref[e])
        mixture += probs[:, e : e + 1] * pair_out
        grad = jnp.sum(g * pair_out, axis=1, keepdims=True)
        pgrad = jnp.where(spot == e, grad, pgrad)
        moe_in += mm(hot, ein_ref[e])
    mid = mid_ref[...]
    block_ref[...] = (mid + sout_ref[...] + mixture).astype(bf16)
    inner = jnp.sum(pgrad * probs, axis=1, keepdims=True)
    lgrad = (probs * (pgrad - inner)).astype(bf16)
    h2_grad = moe_in + mm_nt(lgrad, wr_ref[...]) + sin_ref[...]
    r2 = lax.rsqrt(jnp.mean(mid * mid, axis=1, keepdims=True) + norm_eps)
    n2 = mid * r2
    d2 = h2_grad * gains_ref[5:6, :]
    mid_grad = g + r2 * (d2 - n2 * jnp.mean(d2 * n2, axis=1, keepdims=True))
    midb = mid_grad.astype(bf16)
    midg_ref[...] = mid_grad
    midb_ref[...] = midb
    og_ref[...] = mm_nt(midb, wo_ref[0]).astype(bf16)
    gsum = jnp.sum(h2_grad * n2, axis=0, keepdims=True)
    rsum = mm_tn(lgrad, h2_ref[...])[:8]

    @pl.when(step == 0)
    def _():
        gain_ref[...] = jnp.zeros_like(gain_ref)
        rgrad_ref[...] = jnp.zeros_like(rgrad_ref)

    gain_ref[0:1, :] += gsum
    rgrad_ref[...] += rsum

    @pl.when(step == pl.num_programs(0) - 1)
    def _():
        for copy in exchange():
            copy.wait()


def combine(mid, sout, sin, g, h2, probs, place_col, eout, ein, gains, wr, full, part):
    seq, width = mid.shape
    tile = 256
    by_rows = pl.BlockSpec((tile, width), lambda i: (i, 0))
    lanes = pl.BlockSpec((tile, 128), lambda i: (i, 0))
    return pl.pallas_call(
        combine_kernel,
        grid=(seq // tile,),
        in_specs=[
            by_rows, by_rows, by_rows, by_rows, by_rows, lanes, lanes,
            once(eout.shape), once(ein.shape), once(gains.shape), once(wr.shape),
            pl.BlockSpec((1, width, width), lambda i: (3, 0, 0), pipeline_mode=pl.Buffered(1)),
            ANY,
        ],
        out_specs=[
            by_rows, by_rows, by_rows, by_rows, whole_spec((8, width)), whole_spec((8, width)), ANY,
        ],
        out_shape=[
            jax.ShapeDtypeStruct((seq, width), bf16),
            jax.ShapeDtypeStruct((seq, width), f32),
            jax.ShapeDtypeStruct((seq, width), bf16),
            jax.ShapeDtypeStruct((seq, width), bf16),
            jax.ShapeDtypeStruct((8, width), f32),
            jax.ShapeDtypeStruct((8, width), f32),
            jax.ShapeDtypeStruct(part.shape, bf16),
        ],
        scratch_shapes=pair_sems(part.shape[0]),
        compiler_params=params(("arbitrary",), collective_id=5, has_side_effects=True),
        cost_estimate=pl.CostEstimate(
            flops=11_000_000_000, bytes_accessed=30_000_000, transcendentals=0
        ),
        name="combine",
    )(mid, sout, sin, g, h2, probs, place_col, eout, ein, gains, wr, full, part)


def backward_kernel(
    exps, shds,
    qkv_ref, og_ref, lse_ref, bidr_ref, bidc_ref, tok_ref, midg_ref, o_ref, midb_ref, w_ref,
    gains_ref, gain2_ref, rgrad_ref, lb_ref, part_ref,
    igrad_ref, sw_ref, sa_ref, sb_ref, st_ref,
    dk_s, dv_s, h1t_s, ot_s, grad_s, stack_s, pair_s, plane_s, r_s, zr_s, fw_s,
    la_s, qa_s, qb_s, za_s, zb_s, fa_s, fb_s, tiny_s, tpair_s, tplane_s, tz_s,
    a_send, a_recv, pair_send, pair_recv, p_send, p_recv, r_send, r_recv, f_own, f_send, f_recv,
    line_send, line_recv, last_own, last_send, last_recv, t_send, t_recv, tp_send, tp_recv,
):
    step = pl.program_id(0)
    columns, layers = others("exp", exps), others("shd", shds)
    group = lax.axis_index("grp")
    core = lax.rem(group, 2)
    partner = {"grp": lax.bitwise_xor(group, 1)}
    seq, width = tok_ref.shape
    tile = 256
    pieces = width // 128
    deep = width // exps
    early = [(j + 1) % shds for j in range(shds)]

    def chunk(j):
        return plane_copies(
            exps, lambda c: part_ref.at[c, layers[j]], la_s.at[j], a_send.at[j], a_recv.at[j]
        )

    def chunk_line(j):
        return send(
            qa_s.at[j], za_s.at[j], line_send.at[0, j], line_recv.at[0, j], {"shd": layers[j]}
        )

    def chunk_sum(j, landed):
        value = landed[0].astype(f32)
        for k in range(1, exps):
            value = value + landed[k].astype(f32)
        qa_s[j] = value.astype(bf16)
        if j:
            chunk_line(j).start()

    def line(part_s, landed_s, kind):
        return [
            send(
                part_s.at[layers[k]], landed_s.at[k],
                line_send.at[kind, k], line_recv.at[kind, k], {"shd": layers[k]},
            )
            for k in range(1, shds)
        ]

    def plane_rows(k):
        return pl.ds(pl.multiple_of(columns[k] * deep, 16), deep)

    def pair_copy(p):
        return send(stack_s.at[p], pair_s.at[p // 2], pair_send.at[p // 2], pair_recv.at[p // 2], partner)

    def plane_copy(p):
        return [
            send(
                stack_s.at[p, :, plane_rows(k), :], plane_s.at[p // 2, k],
                p_send.at[p // 2, k], p_recv.at[p // 2, k], {"exp": columns[k]},
            )
            for k in range(1, exps)
        ]

    def line_copy(p):
        return [
            send(
                r_s.at[p // 2, layers[k]], zr_s.at[p // 2, k],
                r_send.at[p // 2, k], r_recv.at[p // 2, k], {"shd": layers[k]},
            )
            for k in range(1, shds)
        ]

    def final_copy(p):
        at = sw_ref.at[:, :, pl.ds(pl.multiple_of(p * 128, 128), 128)]
        return [
            pltpu.make_async_copy(fw_s.at[p // 2], at, f_own.at[p // 2]),
            send(fw_s.at[p // 2], at, f_send.at[p // 2], f_recv.at[p // 2], partner),
        ]

    def start(copies):
        for copy in copies:
            copy.start()

    def summing(p):
        return jnp.logical_and(p >= 0, core == p % 2)

    def to_pair(p):
        @pl.when(core != p % 2)
        def _():
            pair_copy(p).start()

    def to_plane(p):
        @pl.when(summing(p))
        def _():
            pair_copy(p).wait_recv()
            for i in range(4):
                stack_s[p, i] = (stack_s[p, i].astype(f32) + pair_s[p // 2, i].astype(f32)).astype(bf16)
            start(plane_copy(p))

    def to_line(p):
        @pl.when(summing(p))
        def _():
            for copy in plane_copy(p):
                copy.wait_recv()
            for i in range(4):
                value = stack_s[p, i, plane_rows(0), :].astype(f32)
                for k in range(1, exps):
                    value = value + plane_s[p // 2, k, i].astype(f32)
                r_s[p // 2, :, i] = value.astype(bf16).reshape(shds, deep // shds, 128)
            start(line_copy(p))

    def to_final(p):
        @pl.when(summing(p))
        def _():
            for copy in line_copy(p):
                copy.wait_recv()
            value = r_s[p // 2, layers[0]].astype(f32)
            for k in range(1, shds):
                value = value + zr_s[p // 2, k].astype(f32)
            fw_s[p // 2] = value
            start(final_copy(p))

    def line_total(landed_s, part_s):
        value = part_s[layers[0]].astype(f32)
        for k in range(1, shds):
            value = value + landed_s[k].astype(f32)
        return value

    def finals(kind, part_s, out_ref):
        return [
            pltpu.make_async_copy(part_s, out_ref.at[core], last_own.at[kind]),
            send(part_s, out_ref.at[core], last_send.at[kind], last_recv.at[kind], partner),
        ]

    @pl.when(step == 0)
    def _():
        greet(
            [{"shd": layer} for layer in layers[1:]]
            + [{"exp": column} for column in columns[1:]]
            + [partner]
        )
        for z in range(shds):
            qb_s[z] = sum([lb_ref[k, z].astype(f32) for k in range(1, exps)], lb_ref[0, z].astype(f32)).astype(bf16)
        start(line(qb_s, zb_s, 1))
        for row in range(0, seq, tile):
            x = tok_ref[row : row + tile, :].astype(f32)
            r1 = lax.rsqrt(jnp.mean(x * x, axis=1, keepdims=True) + norm_eps)
            h1t_s[:, row : row + tile] = (x * r1 * gains_ref[4:5, :]).astype(bf16).T
            ot_s[:, row : row + tile] = o_ref[row : row + tile, :].T
        grad_s[...] = jnp.zeros_like(grad_s)

    for turn, j in enumerate(early):

        @pl.when(step == turn)
        def _():
            start(chunk(j))

        @pl.when(step == turn + 2)
        def _():
            for copy in chunk(j):
                copy.wait()
            chunk_sum(j, la_s.at[j])

    @pl.when(step == shds)
    def _():
        for copy in line(qb_s, zb_s, 1):
            copy.wait()
        fb_s[...] = line_total(zb_s, qb_s)
        start(finals(1, fb_s, sb_ref))

    qs = qkv_ref[0] * jnp.asarray(0.125, bf16)
    k = qkv_ref[1]
    v = qkv_ref[2]
    kt = k.T
    og = og_ref[...]
    lane = lax.broadcasted_iota(jnp.int32, (tile, 128), 1)
    dk_s[...] = jnp.zeros_like(dk_s)
    dv_s[...] = jnp.zeros_like(dv_s)
    dqs = []
    for q0 in range(0, seq, tile):
        kl = min(seq, q0 + 2 * tile)
        qt, ot = qs[q0 : q0 + tile], og[q0 : q0 + tile]
        allowed = bidc_ref[q0:kl, :] <= bidr_ref[0:1, q0 : q0 + tile]
        parts = []
        for head in range(2):
            own = (lane // 64) == head
            qm = jnp.where(own, qt, jnp.zeros_like(qt))
            om = jnp.where(own, ot, jnp.zeros_like(ot))
            lse = lse_ref[0, head : head + 1, q0 : q0 + tile]
            spans = ([(0, q0)] if q0 else []) + [(q0, kl)]
            kept = []
            delta = jnp.zeros((1, tile), f32)
            for low, high in spans:
                s = mm_nt(k[low:high], qm)
                if low == q0:
                    s = jnp.where(allowed, s, masked_score)
                p = jnp.exp(s - lse)
                dp = mm_nt(v[low:high], om)
                delta = delta + jnp.sum(p * dp, axis=0, keepdims=True)
                kept.append((low, high, p, dp))
            dq = jnp.zeros((64, tile), f32)
            for low, high, p, dp in kept:
                ds = (p * (dp - delta)).astype(bf16)
                dv_s[low:high, :] += mm(p.astype(bf16), om)
                dk_s[low:high, :] += mm(ds, qm)
                dq = dq + mm(kt[64 * head : 64 * head + 64, low:high], ds)
            parts.append(dq)
        dqs.append((jnp.concatenate(parts, axis=0).T * 0.125).astype(bf16))
        if q0 == tile:
            to_plane(step - 1)
    dqkv = [jnp.concatenate(dqs, axis=0), dk_s[...].astype(bf16), dv_s[...].astype(bf16)]
    to_final(step - 4)
    to_line(step - 3)
    wide = mm(h1t_s[...], jnp.concatenate(dqkv, axis=1)).astype(bf16)
    for i in range(3):
        stack_s[step, i] = wide[:, 128 * i : 128 * i + 128]
    stack_s[step, 3] = mm(ot_s[...], midb_ref[...]).astype(bf16)
    to_pair(step)
    for row in range(0, seq, tile):
        rows = slice(row, row + tile)
        grad_s[rows, :] += (
            mm_nt(dqkv[0][rows], w_ref[0]) + mm_nt(dqkv[1][rows], w_ref[1]) + mm_nt(dqkv[2][rows], w_ref[2])
        )

    @pl.when(step == pieces - 1)
    def _():
        to_line(pieces - 3)
        to_final(pieces - 4)
        to_plane(pieces - 1)
        gain = jnp.zeros((1, width), f32)
        for row in range(0, seq, tile):
            rows = slice(row, row + tile)
            x = tok_ref[rows, :].astype(f32)
            r1 = lax.rsqrt(jnp.mean(x * x, axis=1, keepdims=True) + norm_eps)
            n1 = x * r1
            grad = grad_s[rows, :]
            gain = gain + jnp.sum(grad * n1, axis=0, keepdims=True)
            d1 = grad * gains_ref[4:5, :]
            igrad_ref[rows, :] = midg_ref[rows, :] + r1 * (d1 - n1 * jnp.mean(d1 * n1, axis=1, keepdims=True))
        spot = lax.broadcasted_iota(jnp.int32, (8, width), 0)
        small = jnp.where(spot < 4, rgrad_ref[...], jnp.where(spot == 4, gain, gain2_ref[0:1, :]))
        tiny_s[...] = small
        tswap = send(tiny_s, tpair_s, t_send, t_recv, partner)
        tswap.start()
        to_line(pieces - 2)
        to_final(pieces - 3)
        to_line(pieces - 1)
        tswap.wait()
        tpair_s[...] += tiny_s[...]
        tplane = [
            send(tpair_s, tplane_s.at[k], tp_send.at[k], tp_recv.at[k], {"exp": columns[k]})
            for k in range(1, exps)
        ]
        start(tplane)
        to_final(pieces - 2)
        for copy in tplane:
            copy.wait()
        value = qa_s[0].astype(f32)
        for j in range(1, shds):
            chunk_line(j).wait()
            value = value + za_s[j].astype(f32)
        fa_s[...] = value
        start(finals(0, fa_s, sa_ref))
        tz_s[0] = sum([tplane_s[k] for k in range(1, exps)], tpair_s[...])
        tline = [
            send(
                tz_s.at[0], tz_s.at[k], line_send.at[2, k], line_recv.at[2, k], {"shd": layers[k]}
            )
            for k in range(1, shds)
        ]
        start(tline)
        to_final(pieces - 1)
        for copy in tline:
            copy.wait()
        st_ref[...] = sum([tz_s[k] for k in range(1, shds)], tz_s[0])
        for p in range(pieces):

            @pl.when(core == p % 2)
            def _():
                for copy in plane_copy(p) + line_copy(p) + final_copy(p)[1:]:
                    copy.wait_send()
                final_copy(p)[0].wait()

            @pl.when(core != p % 2)
            def _():
                pair_copy(p).wait_send()
                final_copy(p)[1].wait_recv()

        for copy in finals(1, fb_s, sb_ref) + finals(0, fa_s, sa_ref):
            copy.wait()


def attention_backward(qkv, og, lse, bid_row, bid_col, tokens, midg, o, midb, full, gains, gain2, rgrad, lb, part):
    exps, shds = part.shape[:2]
    seq, width = tokens.shape
    rows = part.shape[2]
    pairs = width // 128
    half = pairs // 2
    big = lambda *shape: pltpu.VMEM(shape, bf16)
    wide = lambda *shape: pltpu.VMEM(shape, f32)
    sems = lambda *n: pltpu.SemaphoreType.DMA(n)
    a, b = part.shape[2:], lb.shape[2:]
    return pl.pallas_call(
        functools.partial(backward_kernel, exps, shds),
        grid=(pairs,),
        in_specs=[
            pl.BlockSpec((3, seq, 128), lambda i: (0, 0, i)),
            pl.BlockSpec((seq, 128), lambda i: (0, i)),
            pl.BlockSpec((1, 8, seq), lambda i: (i, 0, 0)),
            once(bid_row.shape),
            once(bid_col.shape),
            once(tokens.shape),
            once(midg.shape),
            once(o.shape),
            pl.BlockSpec((seq, 128), lambda i: (0, i)),
            pl.BlockSpec((3, width, 128), lambda i: (0, 0, i)),
            once(gains.shape),
            once(gain2.shape),
            once(rgrad.shape),
            once(lb.shape),
            ANY,
        ],
        out_specs=[once((seq, width)), ANY, ANY, ANY, once((8, width))],
        out_shape=[
            jax.ShapeDtypeStruct((seq, width), f32),
            jax.ShapeDtypeStruct((4, rows, width), f32),
            jax.ShapeDtypeStruct((2,) + a, f32),
            jax.ShapeDtypeStruct((2,) + b, f32),
            jax.ShapeDtypeStruct((8, width), f32),
        ],
        scratch_shapes=[
            wide(seq, 128),
            wide(seq, 128),
            big(width, seq),
            big(width, seq),
            wide(seq, width),
            big(pairs, 4, width, 128),
            big(half, 4, width, 128),
            big(half, exps, 4, width // exps, 128),
            big(half, shds, 4, rows, 128),
            big(half, shds, 4, rows, 128),
            wide(half, 4, rows, 128),
            big(shds, exps, *a),
            big(shds, *a),
            big(shds, *b),
            big(shds, *a),
            big(shds, *b),
            wide(*a),
            wide(*b),
            wide(8, width),
            wide(8, width),
            wide(exps, 8, width),
            wide(shds, 8, width),
            sems(shds, exps), sems(shds, exps), sems(half), sems(half),
            sems(half, exps), sems(half, exps), sems(half, shds), sems(half, shds),
            sems(half), sems(half), sems(half),
            sems(3, shds), sems(3, shds), sems(2), sems(2), sems(2),
            pltpu.SemaphoreType.DMA, pltpu.SemaphoreType.DMA, sems(exps), sems(exps),
        ],
        compiler_params=params(("arbitrary",), collective_id=6, has_side_effects=True),
        cost_estimate=pl.CostEstimate(
            flops=80_000_000_000, bytes_accessed=30_000_000, transcendentals=12_000_000
        ),
        name="attention_backward",
    )(
        qkv, og, lse, bid_row, bid_col, tokens, midg, o, midb, full,
        gains, gain2, rgrad, lb, part,
    )


def adam_update(weight, moment, square, gradient, step_rate, shrink_rate):
    moment_next = beta_one * moment + (1.0 - beta_one) * gradient
    square_next = beta_two * square + (1.0 - beta_two) * gradient * gradient
    direction = moment_next / first_fix / (jnp.sqrt(square_next / second_fix) + adam_eps)
    return (weight - step_rate * (direction + shrink_rate * weight), moment_next, square_next)


def adam_kernel(rates, core_ref, w_ref, m_ref, v_ref, own_ref, other_ref, wo_ref, mo_ref, vo_ref):
    shape = w_ref.shape
    high = shape[-2]
    mine = jnp.full(own_ref.shape, core_ref[0], jnp.int32) == pl.program_id(0)
    gradient = jnp.where(mine, own_ref[...].astype(f32), other_ref[...].astype(f32))
    parts = [gradient[i : i + high] for i in range(0, gradient.shape[0], high)]
    gradient = jnp.concatenate(parts, axis=1).reshape(shape)
    wo_ref[...], mo_ref[...], vo_ref[...] = adam_update(
        w_ref[...], m_ref[...], v_ref[...], gradient, *rates
    )


def adam_blocks(kind, state, sums, core, grid, spec, sums_spec):
    return pl.pallas_call(
        functools.partial(adam_kernel, (learning_rates[kind], decay_rates[kind])),
        grid=grid,
        in_specs=[pl.BlockSpec(memory_space=pltpu.SMEM)] + [spec] * 3 + [sums_spec] * 2,
        out_specs=[spec] * 3,
        out_shape=[jax.ShapeDtypeStruct(state[0].shape, f32)] * 3,
        compiler_params=params(("arbitrary",) * len(grid)),
        cost_estimate=pl.CostEstimate(
            flops=20 * state[0].size, bytes_accessed=26 * state[0].size, transcendentals=0
        ),
        name="adam_blocks",
    )(core.reshape(1), *state, *sums)


def pick(array, axis, index):
    return lax.dynamic_index_in_dim(array, index, axis, keepdims=False)


def share(part, groups, core):
    if groups > 2:
        both = jnp.zeros((2,) + part.shape, f32)
        both = lax.dynamic_update_index_in_dim(both, part.astype(f32), core, 0)
        both = lax.psum(both, "grp")
        return pick(both, 0, core), pick(both, 0, 1 - core)
    return part, lax.ppermute(part, "grp", [(i, i ^ 1) for i in range(groups)])


def on_device(
    tokens_in, cotangent, block_ids, expert_ids,
    scales, moment_scales, square_scales, attend, moment_attend, square_attend,
    output, moment_output, square_output, router, moment_router, square_router,
    widener, moment_widener, square_widener, reducer, moment_reducer, square_reducer,
    experts, moment_experts, square_experts, narrower, moment_narrower, square_narrower,
):
    groups, exps, shds = (lax.axis_size(a) for a in ("grp", "exp", "shd"))
    spread = exps * shds
    core = lax.rem(lax.axis_index("grp"), 2)
    _, seq, width = tokens_in.shape
    hidden = reducer.shape[0] * spread
    experts_all = exps * experts.shape[0]
    rows, tall = output.shape[0], reducer.shape[0] // 2
    deep = width // shds
    tokens, g = tokens_in.reshape(seq, width), cotangent.reshape(seq, width)

    def packed(wide, narrow):
        wide = pick(wide.astype(bf16), 0, core)
        narrow = pick(narrow.astype(bf16).reshape(2, -1, width), 0, core)
        blocks = [
            a.reshape(a.shape[0], -1, 256).transpose(1, 0, 2).reshape(-1, 256) for a in (wide, narrow)
        ]
        return jnp.concatenate(blocks, axis=0)

    def gather(part, axes):
        wide = lax.all_gather(part, ("grp",) + axes, axis=0, tiled=False)
        return wide.reshape((groups, -1) + part.shape)[:2]

    mine = jnp.where(
        core == 0,
        attend[:2].astype(bf16),
        jnp.stack([attend[2].astype(bf16), output.astype(bf16)]),
    )
    tiny = jnp.concatenate([router, scales.T], axis=1).astype(bf16)
    tiny = jnp.pad(tiny, ((0, 0), (0, 128 - tiny.shape[1])))
    expert_weights = gather(packed(experts[0], narrower[0]), ("shd",))
    shared_pack = packed(widener, reducer)

    ids = jnp.pad(expert_ids.reshape(seq, 2).T, ((0, 6), (0, 0)), constant_values=-1)
    bid = block_ids.reshape(1, seq)
    bid_row = jnp.broadcast_to(bid, (8, seq))
    bid_col = jnp.broadcast_to(bid.reshape(seq, 1), (seq, 256))

    lanes = -(-CAP // 128) * 128
    full, wr, packs, g_slots, place_row, place_col = gather_first(
        mine, tiny, shared_pack, g, ids, exps, shds, experts_all, CAP
    )
    qkv, lse, o, mid, h2, probs, probst, gains, g_landed = attention_forward(
        tokens, bid_row, bid_col, full, wr, g_slots
    )
    shared_weights = gather(packs, ("shd",)).reshape((2, shds) + packs.shape)
    slot_rows, chosen = dispatch(h2, place_row, probst, experts_all, CAP, lanes)
    eout, back, part = routed(slot_rows, chosen, g_landed, expert_weights, hidden)
    part = lax.psum_scatter(part, "shd", scatter_dimension=0, tiled=False)
    sout, sin, part_a, part_b, ein = ffn(
        h2, g, shared_weights, back, hidden, f32, 256, "shared"
    )
    part_a = part_a.reshape(exps, shds, rows, hidden)
    part_b = part_b.reshape(exps, shds, tall, width)
    block_out, mid_grad, midb, og, gain_two, rgrad, landed_b = combine(
        mid, sout, sin, g, h2, probs, place_col, eout, ein, gains, wr, full, part_b
    )
    input_grad, sum_w, sum_a, sum_b, sum_t = attention_backward(
        qkv, og, lse, bid_row, bid_col, tokens, mid_grad, o, midb, full,
        gains, gain_two, rgrad, landed_b, part_a,
    )
    if groups > 2:
        sum_w, sum_a, sum_b, sum_t = (
            0.5 * lax.psum(v, "grp") for v in (sum_w, sum_a, sum_b, sum_t)
        )
    expert_sums = share(part, groups, core)
    wide_state = [v[0] for v in (experts, moment_experts, square_experts)]
    new_experts = adam_blocks(
        6, wide_state, expert_sums, core, (2, hidden // 512),
        pl.BlockSpec((1, deep, 512), lambda c, b: (c, 0, b)),
        pl.BlockSpec((2 * deep, 256), lambda c, b: (b, 0)),
    )
    narrow_state = [v[0] for v in (narrower, moment_narrower, square_narrower)]
    high = narrower.shape[1] // 2
    across = width // 256
    skip = hidden // 256 * deep // (across * high)
    new_narrower = adam_blocks(
        7, narrow_state, expert_sums, core, (2, 1),
        pl.BlockSpec((high, width), lambda c, b: (c, b)),
        pl.BlockSpec((across * high, 256), lambda c, b: (skip + b, 0)),
    )
    shard = lax.axis_index("exp") * shds + lax.axis_index("shd")
    sum_t = lax.dynamic_slice_in_dim(sum_t, shard * rows, rows, 1)
    grads = (
        sum_t[4:6],
        sum_w[:3],
        sum_w[3],
        sum_t[:experts_all].T,
        sum_a,
        sum_b.reshape(reducer.shape),
    )
    masters = (scales, attend, output, router, widener, reducer)
    moments = (
        moment_scales, moment_attend, moment_output, moment_router,
        moment_widener, moment_reducer,
    )
    squares = (
        square_scales, square_attend, square_output, square_router,
        square_widener, square_reducer,
    )
    results = [block_out.reshape(tokens_in.shape), input_grad.reshape(tokens_in.shape)]
    for kind in range(6):
        results.extend(
            adam_update(
                masters[kind], moments[kind], squares[kind], grads[kind],
                learning_rates[kind], decay_rates[kind],
            )
        )
    results.extend(v[None] for v in new_experts)
    results.extend(v[None] for v in new_narrower)
    return tuple(results)


def solution(mesh):
    tokens = P(("grp", "exp", "shd"), None, None)
    both = ("exp", "shd")
    kinds = (
        P(None, both), P(None, both, None), P(both, None), P(both, None),
        P(None, both, None), P(both, None), P("exp", None, "shd", None), P("exp", "shd", None),
    )
    thrice = tuple(kind for kind in kinds for _ in range(3))
    return jax.shard_map(
        on_device,
        mesh=mesh,
        in_specs=(tokens, tokens, P(("grp", "exp", "shd"), None), tokens) + thrice,
        out_specs=(tokens, tokens) + thrice,
        check_vma=False,
    )
```

profile of v0, /device:TPU:0, one launch (start us, length us, event | category | flops | bytes accessed | tf_op | source)
XLA Modules:
  0.0 413.9 jit_solution(1258774358344660650)
XLA Ops:
  7.2 0.0 all-gather.7.cloned.1.call-start
  7.3 1.6 dynamic-slice_convert_fusion
  8.9 0.2 copy.74
  9.1 0.2 copy.70
  9.3 0.1 convert_element_type.29
  9.4 0.2 copy.71
  9.6 0.2 copy.72
  9.8 1.1 pad_maximum_fusion
  10.9 0.0 all-gather.7.cloned.1.call-update
  10.9 0.0 all-gather.5.cloned.1.call-start
  11.0 0.1 copy.67
  11.1 1.0 dynamic-slice_convert_fusion.1
  12.4 0.6 pad.8.tiny_ref
  13.1 0.6 pad.9.ids_ref
  13.7 0.7 pad_maximum_fusion.1.pack_ref
  14.4 0.7 slice_select_fusion.mine_ref
  15.1 45.8 %gather_first.1 = (bf16[4,768,768]{2,1,0:T(8,128)(2,1)}, bf16[768,128]{1,0:T(8,128)(2,1)}, bf16[4,576,256]{2,1,0:T(8,128)(2,1)}, bf16[4,576,768]{2,1,0:T(8,128)(...) custom-call(bf16[2,48,768]{2,1,0:T(8,128)(2,1)} %slice_select_fusion.mine_ref, bf16[48,128]{1,0:T(8,128)(2,1)} %pad.8.tiny_ref, ...), custom_call_target="tpu_custom_call" | custom-call | flops 40000000000 | bytes 10000000 | tf_op jit(solution)/shard_map/gather_first/pallas_call | solution.py:206
  60.9 0.0 all-gather.5.cloned.1.call-update
  60.9 0.2 reduce-scatter.2.cloned.1.call-start
  61.2 0.6 broadcast_in_dim.31.bidr_ref
  61.8 1.2 broadcast_in_dim.32.bidc_ref
  63.0 48.0 %attention_forward.1 = (bf16[3,1024,768]{2,1,0:T(8,128)(2,1)}, f32[6,8,1024]{2,1,0:T(8,128)}, bf16[1024,768]{1,0:T(8,128)(2,1)}, f32[1024,768]{1,0:T(8,128)}, bf...) custom-call(bf16[1024,768]{1,0:T(8,128)(2,1)} %bitcast.108, ...), custom_call_target="tpu_custom_call" | custom-call | flops 30000001024 | bytes 20000000 | tf_op jit(solution)/shard_map/attention_forward/pallas_call | solution.py:326
  111.0 8.1 %dispatch.1 = (bf16[4,576,768]{2,1,0:T(8,128)(2,1)}, f32[4,8,640]{2,1,0:T(8,128)}) custom-call(bf16[1024,768]{1,0:T(8,128)(2,1)} %get-tuple-element.73.h2_ref.x_ref, s32[16,1024]{1,0:T(8,128)} %get-tuple-element.75.place_ref, f32[16,1024]{1,0:T(8,128)} %get-tuple-element.76.probst_ref), custom_call_target="tpu_custom_call" | custom-call | flops 5000000000 | bytes 6000000 | tf_op jit(solution)/shard_map/dispatch/pallas_call | solution.py:395
  119.0 89.7 %routed.1 = (bf16[4,576,768]{2,1,0:T(8,128)(2,1)}, bf16[4,576,768]{2,1,0:T(8,128)(2,1)}, bf16[4,2304,256]{2,1,0:T(8,128)(2,1)}) custom-call(bf16[4,576,768]{2,1,0:T(8,128)(2,1)} %get-tuple-element.77.rows_ref, f32[4,8,640]{2,1,0:T(8,128)} %get-tuple-element.78.chosen_ref, bf16[4,576,768]{2,1,0:T(8,128)(2,1)} %get-tuple-element.79.grads_ref, ...), custom_call_target="tpu_custom_call" | custom-call | flops 65229815808 | bytes 40000000 | tf_op jit(solution)/shard_map/routed/pallas_call | solution.py:584
  208.8 0.0 reduce-scatter.2.cloned.1.call-update
  208.8 0.0 all-gather.5.cloned.1.call-done
  208.8 48.1 %shared.1 = (f32[1024,768]{1,0:T(8,128)}, f32[1024,768]{1,0:T(8,128)}, bf16[768,2048]{1,0:T(8,128)(2,1)}, bf16[16,64,768]{2,1,0:T(8,128)(2,1)}, bf16[4,576,768]{2,1,0:T(8,128)(2,1)}) custom-call(bf16[1024,768]{1,0:T(8,128)(2,1)} %get-tuple-element.73.h2_ref.x_ref, bf16[1024,768]{1,0:T(8,128)(2,1)} %bitcast.106, bf16[2,4,4,576,256]{4,3,2,1,0:T(8,128)(2,1)} %bitcast.99, ...), custom_call_target="tpu_custom_call" | custom-call | flops 28991029248 | bytes 25165824 | tf_op jit(solution)/shard_map/shared/pallas_call | solution.py:749
  256.9 27.5 %combine.1 = (bf16[1024,768]{1,0:T(8,128)(2,1)}, f32[1024,768]{1,0:T(8,128)}, bf16[1024,768]{1,0:T(8,128)(2,1)}, bf16[1024,768]{1,0:T(8,128)(2,1)}, f32[8,768]{1...) custom-call(f32[1024,768]{1,0:T(8,128)} %get-tuple-element.72.mid_ref, ...), custom_call_target="tpu_custom_call" | custom-call | flops 11000000512 | bytes 30000000 | tf_op jit(solution)/shard_map/combine/pallas_call | solution.py:871
  284.4 0.0 copy-start.27
  284.5 0.0 copy-start.22
  284.5 0.0 copy-start.24
  284.5 0.0 copy-start.18
  284.5 0.0 copy-start.19
  284.6 90.9 %attention_backward.1 = (f32[1024,768]{1,0:T(8,128)}, f32[4,48,768]{2,1,0:T(8,128)}, f32[2,48,2048]{2,1,0:T(8,128)}, f32[2,64,768]{2,1,0:T(8,128)}, f32[8,768]{1,0:T(8,128)}) custom-call(bf16[3,1024,768]{2,1,0:T(8,128)(2,1)} %get-tuple-element.90.qkv_ref, bf16[1024,768]{1,0:T(8,128)(2,1)} %get-tuple-element.91.og_ref, ...), custom_call_target="tpu_custom_call" | custom-call | flops 80000000000 | bytes 30000000 | tf_op jit(solution)/shard_map/attention_backward/pallas_call | solution.py:1203
  375.5 0.9 constant_dynamic-slice_fusion
  376.4 0.6 multiply_subtract_fusion.5
  377.0 0.6 multiply_subtract_fusion.4
  377.7 1.7 multiply_subtract_fusion.3
  379.4 0.9 collective-permute-start
  380.4 2.5 multiply_subtract_fusion.2
  382.8 1.3 multiply_subtract_fusion.1
  384.1 1.8 multiply_subtract_fusion
  385.9 1.0 copy-done.1
  387.0 11.0 %adam_blocks.2 = (f32[2,192,2048]{2,1,0:T(8,128)}, f32[2,192,2048]{2,1,0:T(8,128)}, f32[2,192,2048]{2,1,0:T(8,128)}) custom-call(s32[1]{0:T(128)} %bitcast.28.core_ref, f32[2,192,2048]{2,1,0:T(8,128)} %bitcast.73, f32[2,192,2048]{2,1,0:T(8,128)} %bitcast.81, f32[2,192,2048]{2,1,0:T(8,128)} %bitcast.82, bf16[2304,256]{1,0:T(8,128)(2,1)} %bitcast.75, ...), custom_call_target="tpu_custom_call" | custom-call | flops 15728640 | bytes 20447232 | tf_op jit(solution)/shard_map/adam_blocks/pallas_call | solution.py:1291
  398.0 5.1 %adam_blocks.3 = (f32[512,768]{1,0:T(8,128)}, f32[512,768]{1,0:T(8,128)}, f32[512,768]{1,0:T(8,128)}) custom-call(s32[1]{0:T(128)} %bitcast.28.core_ref, f32[512,768]{1,0:T(8,128)} %bitcast.71, f32[512,768]{1,0:T(8,128)} %bitcast.84, f32[512,768]{1,0:T(8,128)} %bitcast.85, bf16[2304,256]{1,0:T(8,128)(2,1)} %bitcast.76, bf16[2304,256]{1,0:T(8,128)(2,1)} %copy-done.1), custom_call_target="tpu_custom_call" | custom-call | flops 7864320 | bytes 10223616 | tf_op jit(solution)/shard_map/adam_blocks/pallas_call | solution.py:1291
  403.1 1.1 copy.77
  404.2 1.3 copy-done.2
  405.5 1.7 copy.78
  (69 shorter events, 0.4 us)
Async XLA Ops:
  7.2 111.8 %all-gather.7.cloned.1.call-start = ((), (), s32[]{:S(2)}) async-start(), calls=%async_computation.3 | async-start | bytes 10616832 | tf_op jit(solution)/shard_map/all_gather | solution.py:1344
  7.3 2.0 copy-start
  9.6 1.4 copy-start.21
  9.6 1.4 copy-start.26
  9.8 2.5 copy-start.6
  10.9 1.5 copy-start.3
  10.9 2.2 copy-start.23
  10.9 3.5 copy-start.13
  10.9 197.9 %all-gather.5.cloned.1.call-start = ((), (), s32[]{:S(2)}) async-start(), calls=%async_computation.2 | async-start | bytes 10616832 | tf_op jit(solution)/shard_map/all_gather | solution.py:1344
  15.1 46.1 %copy-start.20 = (s32[1,1024]{1,0:T(1,128)S(1)}, s32[1,1024]{1,0:T(1,128)}, u32[]{:S(2)}) copy-start(s32[1,1024]{1,0:T(1,128)} %param.30) | copy-start | bytes 12292
  60.9 318.5 %reduce-scatter.2.cloned.1.call-start = ((), (), s32[]{:S(2)}) async-start(), calls=%async_computation.1 | async-start | bytes 5898240 | tf_op jit(solution)/shard_map/reduce_scatter | solution.py:1372
  284.4 92.0 %copy-start.27 = (f32[2,48]{1,0:T(2,128)S(1)}, f32[2,48]{1,0:T(2,128)}, u32[]{:S(2)}) copy-start(f32[2,48]{1,0:T(2,128)} %param.32) | copy-start | bytes 1156
  284.5 92.0 %copy-start.28 = (f32[2,48]{1,0:T(2,128)S(1)}, f32[2,48]{1,0:T(2,128)}, u32[]{:S(2)}) copy-start(f32[2,48]{1,0:T(2,128)} %param.33) | copy-start | bytes 1156
  284.5 92.0 %copy-start.29 = (f32[2,48]{1,0:T(2,128)S(1)}, f32[2,48]{1,0:T(2,128)}, u32[]{:S(2)}) copy-start(f32[2,48]{1,0:T(2,128)} %param.34) | copy-start | bytes 1156
  284.5 92.6 %copy-start.22 = (f32[48,4]{0,1:T(4,128)S(1)}, f32[48,4]{0,1:T(4,128)}, u32[]{:S(2)}) copy-start(f32[48,4]{0,1:T(4,128)} %param.41) | copy-start | bytes 2308
  284.5 92.6 %copy-start.24 = (f32[48,4]{0,1:T(4,128)S(1)}, f32[48,4]{0,1:T(4,128)}, u32[]{:S(2)}) copy-start(f32[48,4]{0,1:T(4,128)} %param.42) | copy-start | bytes 2308
  284.5 92.5 %copy-start.25 = (f32[48,4]{0,1:T(4,128)S(1)}, f32[48,4]{0,1:T(4,128)}, u32[]{:S(2)}) copy-start(f32[48,4]{0,1:T(4,128)} %param.43) | copy-start | bytes 2308
  284.5 93.1 %copy-start.14 = (f32[48,768]{1,0:T(8,128)S(1)}, f32[48,768]{1,0:T(8,128)}, u32[]{:S(2)}) copy-start(f32[48,768]{1,0:T(8,128)} %param.38) | copy-start | bytes 442372
  284.5 93.1 %copy-start.18 = (f32[48,768]{1,0:T(8,128)S(1)}, f32[48,768]{1,0:T(8,128)}, u32[]{:S(2)}) copy-start(f32[48,768]{1,0:T(8,128)} %param.39) | copy-start | bytes 442372
  284.5 93.1 %copy-start.19 = (f32[48,768]{1,0:T(8,128)S(1)}, f32[48,768]{1,0:T(8,128)}, u32[]{:S(2)}) copy-start(f32[48,768]{1,0:T(8,128)} %param.40) | copy-start | bytes 442372
  284.6 95.8 %copy-start.7 = (f32[128,768]{1,0:T(8,128)S(1)}, f32[128,768]{1,0:T(8,128)}, u32[]{:S(2)}) copy-start(f32[128,768]{1,0:T(8,128)} %param.47) | copy-start | bytes 1179652
  284.6 95.8 %copy-start.17 = (f32[128,768]{1,0:T(8,128)S(1)}, f32[128,768]{1,0:T(8,128)}, u32[]{:S(2)}) copy-start(f32[128,768]{1,0:T(8,128)} %param.48) | copy-start | bytes 1179652
  375.5 7.3 %copy-start.4 = (f32[3,48,768]{2,1,0:T(8,128)S(1)}, f32[3,48,768]{2,1,0:T(8,128)}, u32[]{:S(2)}) copy-start(f32[3,48,768]{2,1,0:T(8,128)} %param.35) | copy-start | bytes 1327108
  375.5 7.3 %copy-start.12 = (f32[4,48,768]{2,1,0:T(8,128)S(1)}, f32[4,48,768]{2,1,0:T(8,128)}, u32[]{:S(2)}) copy-start(f32[4,48,768]{2,1,0:T(8,128)} %get-tuple-element.102) | copy-start | bytes 1769476
  375.5 7.3 %copy-start.15 = (f32[3,48,768]{2,1,0:T(8,128)S(1)}, f32[3,48,768]{2,1,0:T(8,128)}, u32[]{:S(2)}) copy-start(f32[3,48,768]{2,1,0:T(8,128)} %param.36) | copy-start | bytes 1327108
  375.5 7.3 %copy-start.16 = (f32[3,48,768]{2,1,0:T(8,128)S(1)}, f32[3,48,768]{2,1,0:T(8,128)}, u32[]{:S(2)}) copy-start(f32[3,48,768]{2,1,0:T(8,128)} %param.37) | copy-start | bytes 1327108
  379.4 6.5 %collective-permute-start = (bf16[2304,256]{1,0:T(8,128)(2,1)}, bf16[2304,256]{1,0:T(8,128)(2,1)S(1)}, u32[]{:S(2)}, u32[]{:S(2)}) collective-permute-start(bf16[2304,256]{1,0:T(8,128)(2,1)} %bitcast.74), channel_id=1, source_target_pairs={{0,16},{16,0},{1,17},{17,1},{2,18},{18,2},{3,19},{19,3},{4,20},{20... | collective-permute-start | bytes 3538952 | tf_op jit(solution)/shard_map/ppermute | solution.py:1315
  380.3 3.8 copy-start.8
  380.3 3.8 copy-start.9
  380.4 3.8 copy-start.10
  380.4 3.8 copy-start.11
  385.9 1.0 copy-start.1
  398.0 5.1 %copy-start.5 = (bf16[1024,768]{1,0:T(8,128)(2,1)S(1)}, bf16[1024,768]{1,0:T(8,128)(2,1)}, u32[]{:S(2)}) copy-start(bf16[1024,768]{1,0:T(8,128)(2,1)} %get-tuple-element.89) | copy-start | bytes 4718596
  403.1 2.5 copy-start.2
Sparse Core Ops, SparseCore 0:
  11.0 104.1 all-gather.6
  116.9 90.9 all-gather.4
  210.2 88.7 reduce-scatter.1
where the time goes:
time: 420 us; the launch traced here: 414 us
  Pallas kernels  374 us (89%)
  between operations  14.5 us (3%)
  local copies, waits for them, and re-layouts  12.8 us (3%)
  other arithmetic  11.1 us (3%)
    pallas_call x1, Pallas kernels, attention_backward(): pl.pallas_call(functools.partial(backward_kernel, exps, shds), grid=(pair...  90.9 us
    pallas_call x1, Pallas kernels, routed(): pl.pallas_call(functools.partial(routed_kernel, exps, shds), in_specs=[AN...  89.7 us
    pallas_call x1, Pallas kernels, ffn(): pl.pallas_call(functools.partial(ffn_kernel, tile=tile), grid=(steps,), i...  48.1 us
    pallas_call x1, Pallas kernels, attention_forward(): pl.pallas_call(functools.partial(forward_kernel, exps), grid=(pairs,), in...  48 us
    pallas_call x1, Pallas kernels, gather_first(): pl.pallas_call(functools.partial(gather_kernel, exps, shds), in_specs=[AN...  45.8 us
    pallas_call x1, Pallas kernels, combine(): pl.pallas_call(combine_kernel, grid=(seq // tile,), in_specs=[by_rows, by...  27.5 us
    pallas_call x2, Pallas kernels, adam_blocks(): pl.pallas_call(functools.partial(adam_kernel, (learning_rates[kind], deca...  16.1 us
    sub x6, other arithmetic, adam_update(): weight - step_rate * (direction + shrink_rate * weight)  8.45 us
  transfers between devices with their start and end apart: 4, of which 0 were waited for; matrix products, arithmetic and copies ran while one was open for 4% of the time, Pallas kernels for 87%

commit v1 on v0

--- a/solution.py
+++ b/solution.py
@@ -80,8 +80,8 @@
 
 def gather_kernel(
     exps, shds,
-    mine_ref, tiny_ref, pack_ref, g_ref, ids_ref,
-    full_ref, every_ref, packs_ref, slots_ref, row_ref, col_ref,
+    mine_ref, tiny_ref, pack_ref, g_ref, ids_ref, bid_ref,
+    full_ref, every_ref, packs_ref, slots_ref, row_ref, col_ref, bidc_ref,
     own_sem, z_send, z_recv, p_send, p_recv, c_send, c_recv, k_send, k_recv,
 ):
     columns, layers = others("exp", exps), others("shd", shds)
@@ -138,6 +138,8 @@
     swaps = [send(mine_ref, spots(0, 0)[0], c_send.at[0, 0], c_recv.at[0, 0], partner)]
     swaps[0].start()
     seq = g_ref.shape[0]
+    blocks = bid_ref[...].astype(f32).T[:, 0:1]
+    bidc_ref[...] = jnp.broadcast_to(blocks, bidc_ref.shape).astype(jnp.int32)
     expert = lax.broadcasted_iota(jnp.int32, (16, seq), 0)
     named = (ids_ref[0:1, :] == expert) | (ids_ref[1:2, :] == expert)
     earlier = lax.broadcasted_iota(jnp.int32, (seq, seq), 0) < lax.broadcasted_iota(jnp.int32, (seq, seq), 1)
@@ -199,14 +201,14 @@
         copy.wait()
 
 
-def gather_first(mine, tiny, pack, g, ids, exps, shds, experts_all, cap):
+def gather_first(mine, tiny, pack, g, ids, bids, exps, shds, experts_all, cap):
     _, rows, width = mine.shape
     tall = exps * shds * rows
     sems = lambda *shape: pltpu.SemaphoreType.DMA(shape)
     return pl.pallas_call(
         functools.partial(gather_kernel, exps, shds),
-        in_specs=[ANY, ANY, ANY] + [pl.BlockSpec(memory_space=pltpu.VMEM)] * 2,
-        out_specs=[ANY, ANY, ANY] + [pl.BlockSpec(memory_space=pltpu.VMEM)] * 3,
+        in_specs=[ANY, ANY, ANY] + [pl.BlockSpec(memory_space=pltpu.VMEM)] * 3,
+        out_specs=[ANY, ANY, ANY] + [pl.BlockSpec(memory_space=pltpu.VMEM)] * 4,
         out_shape=[
             jax.ShapeDtypeStruct((4, tall, width), bf16),
             jax.ShapeDtypeStruct((tall, 128), bf16),
@@ -214,6 +216,7 @@
             jax.ShapeDtypeStruct((experts_all, cap, width), bf16),
             jax.ShapeDtypeStruct((16, g.shape[0]), jnp.int32),
             jax.ShapeDtypeStruct((g.shape[0], 128), jnp.int32),
+            jax.ShapeDtypeStruct((g.shape[0], 256), jnp.int32),
         ],
         scratch_shapes=[
             sems(2), sems(shds, 2), sems(shds, 2), sems(shds, exps, 2), sems(shds, exps, 2),
@@ -224,7 +227,7 @@
             flops=40_000_000_000, bytes_accessed=10_000_000, transcendentals=0
         ),
         name="gather_first",
-    )(mine, tiny, pack, g, ids)
+    )(mine, tiny, pack, g, ids, bids)
 
 
 def forward_kernel(
@@ -374,9 +377,9 @@
 def dispatch_kernel(h2_ref, place_ref, probst_ref, rows_ref, chosen_ref):
     expert = pl.program_id(0)
     cap = rows_ref.shape[1]
-    lanes = chosen_ref.shape[2]
     row = place_ref[pl.ds(expert, 1), :]
-    rows_ref[0] = mm(slots_of(row, cap), h2_ref[...]).astype(bf16)
+    hot = slots_of(row, cap)
+    rows_ref[0] = mm(hot, h2_ref[...]).astype(bf16)
     value = probst_ref[pl.ds(expert, 1), :]
     high = value.astype(bf16)
     rest = value - high.astype(f32)
@@ -386,8 +389,9 @@
     pieces = jnp.where(
         spot == 0, high.astype(f32), jnp.where(spot == 1, middle.astype(f32), jnp.where(spot == 2, low.astype(f32), 0.0))
     )
-    chosen = jnp.sum(mm_nt(pieces.astype(bf16), slots_of(row, lanes)), axis=0, keepdims=True)
-    chosen_ref[0] = jnp.broadcast_to(chosen, chosen_ref.shape[1:])
+    chosen = jnp.sum(mm_nt(pieces.astype(bf16), hot), axis=0, keepdims=True)
+    chosen_ref[...] = jnp.zeros_like(chosen_ref)
+    chosen_ref[0, :, :cap] = jnp.broadcast_to(chosen, (8, cap))
 
 
 def dispatch(h2, place_row, probst, experts_all, cap, lanes):
@@ -1357,11 +1361,10 @@
     ids = jnp.pad(expert_ids.reshape(seq, 2).T, ((0, 6), (0, 0)), constant_values=-1)
     bid = block_ids.reshape(1, seq)
     bid_row = jnp.broadcast_to(bid, (8, seq))
-    bid_col = jnp.broadcast_to(bid.reshape(seq, 1), (seq, 256))
 
     lanes = -(-CAP // 128) * 128
-    full, wr, packs, g_slots, place_row, place_col = gather_first(
-        mine, tiny, shared_pack, g, ids, exps, shds, experts_all, CAP
+    full, wr, packs, g_slots, place_row, place_col, bid_col = gather_first(
+        mine, tiny, shared_pack, g, ids, bid_row, exps, shds, experts_all, CAP
     )
     qkv, lse, o, mid, h2, probs, probst, gains, g_landed = attention_forward(
         tokens, bid_row, bid_col, full, wr, g_slots

time: 420 us -> 420 us (level)
  transfers between devices with their start and end apart: 4 -> 4, of which waited for: 0 -> 0; matrix products, arithmetic and copies ran while one was open for 4% -> 3% of each run, Pallas kernels for 87% -> 87%
where the time goes in v1:
time: 420 us; the launch traced here: 414 us
  Pallas kernels  375 us (89%)
  between operations  14.5 us (3%)
  local copies, waits for them, and re-layouts  11.7 us (3%)
  other arithmetic  11.1 us (3%)
    pallas_call x1, Pallas kernels, attention_backward(): pl.pallas_call(functools.partial(backward_kernel, exps, shds), grid=(pair...  90.8 us
    pallas_call x1, Pallas kernels, routed(): pl.pallas_call(functools.partial(routed_kernel, exps, shds), in_specs=[AN...  90.1 us
    pallas_call x1, Pallas kernels, attention_forward(): pl.pallas_call(functools.partial(forward_kernel, exps), grid=(pairs,), in...  48.3 us
    pallas_call x1, Pallas kernels, ffn(): pl.pallas_call(functools.partial(ffn_kernel, tile=tile), grid=(steps,), i...  48.1 us
    pallas_call x1, Pallas kernels, gather_first(): pl.pallas_call(functools.partial(gather_kernel, exps, shds), in_specs=[AN...  46.4 us
    pallas_call x1, Pallas kernels, combine(): pl.pallas_call(combine_kernel, grid=(seq // tile,), in_specs=[by_rows, by...  27.5 us
    pallas_call x2, Pallas kernels, adam_blocks(): pl.pallas_call(functools.partial(adam_kernel, (learning_rates[kind], deca...  16.1 us
    sub x6, other arithmetic, adam_update(): weight - step_rate * (direction + shrink_rate * weight)  8.45 us
  transfers between devices with their start and end apart: 4, of which 0 were waited for; matrix products, arithmetic and copies ran while one was open for 3% of the time, Pallas kernels for 87%

profile of v1, /device:TPU:0, one launch (start us, length us, event | category | flops | bytes accessed | tf_op | source)
XLA Modules:
  0.0 413.9 jit_solution(11172451490380623900)
XLA Ops:
  7.2 0.0 all-gather.7.cloned.1.call-start
  7.3 1.6 dynamic-slice_convert_fusion
  8.9 0.2 copy.74
  9.1 0.2 copy.70
  9.3 0.1 convert_element_type.29
  9.4 0.2 copy.71
  9.6 0.2 copy.72
  9.8 1.1 pad_maximum_fusion
  10.9 0.0 all-gather.7.cloned.1.call-update
  10.9 0.0 all-gather.5.cloned.1.call-start
  11.0 0.1 copy.67
  11.1 1.0 dynamic-slice_convert_fusion.1
  12.5 0.6 pad.8.tiny_ref
  13.1 0.6 pad.9.ids_ref
  13.7 0.7 pad_maximum_fusion.1.pack_ref
  14.4 0.7 slice_select_fusion.mine_ref
  15.1 0.6 broadcast_in_dim.26.bid_ref.bidr_ref
  15.7 46.4 %gather_first.1 = (bf16[4,768,768]{2,1,0:T(8,128)(2,1)}, bf16[768,128]{1,0:T(8,128)(2,1)}, bf16[4,576,256]{2,1,0:T(8,128)(2,1)}, bf16[4,576,768]{2,1,0:T(8,128)(...) custom-call(bf16[2,48,768]{2,1,0:T(8,128)(2,1)} %slice_select_fusion.mine_ref, ...), custom_call_target="tpu_custom_call" | custom-call | flops 40000000000 | bytes 10000000 | tf_op jit(solution)/shard_map/gather_first/pallas_call | solution.py:208
  62.2 0.0 all-gather.5.cloned.1.call-update
  62.2 0.2 reduce-scatter.2.cloned.1.call-start
  62.4 48.3 %attention_forward.1 = (bf16[3,1024,768]{2,1,0:T(8,128)(2,1)}, f32[6,8,1024]{2,1,0:T(8,128)}, bf16[1024,768]{1,0:T(8,128)(2,1)}, f32[1024,768]{1,0:T(8,128)}, bf...) custom-call(bf16[1024,768]{1,0:T(8,128)(2,1)} %bitcast.107, ...), custom_call_target="tpu_custom_call" | custom-call | flops 30000001024 | bytes 20000000 | tf_op jit(solution)/shard_map/attention_forward/pallas_call | solution.py:329
  110.7 8.0 %dispatch.1 = (bf16[4,576,768]{2,1,0:T(8,128)(2,1)}, f32[4,8,640]{2,1,0:T(8,128)}) custom-call(bf16[1024,768]{1,0:T(8,128)(2,1)} %get-tuple-element.75.h2_ref.x_ref, s32[16,1024]{1,0:T(8,128)} %get-tuple-element.77.place_ref, f32[16,1024]{1,0:T(8,128)} %get-tuple-element.78.probst_ref), custom_call_target="tpu_custom_call" | custom-call | flops 5000000000 | bytes 6000000 | tf_op jit(solution)/shard_map/dispatch/pallas_call | solution.py:399
  118.7 90.1 %routed.1 = (bf16[4,576,768]{2,1,0:T(8,128)(2,1)}, bf16[4,576,768]{2,1,0:T(8,128)(2,1)}, bf16[4,2304,256]{2,1,0:T(8,128)(2,1)}) custom-call(bf16[4,576,768]{2,1,0:T(8,128)(2,1)} %get-tuple-element.79.rows_ref, f32[4,8,640]{2,1,0:T(8,128)} %get-tuple-element.80.chosen_ref, bf16[4,576,768]{2,1,0:T(8,128)(2,1)} %get-tuple-element.81.grads_ref, ...), custom_call_target="tpu_custom_call" | custom-call | flops 65229815808 | bytes 40000000 | tf_op jit(solution)/shard_map/routed/pallas_call | solution.py:588
  208.9 0.0 reduce-scatter.2.cloned.1.call-update
  208.9 0.0 all-gather.5.cloned.1.call-done
  208.9 48.1 %shared.1 = (f32[1024,768]{1,0:T(8,128)}, f32[1024,768]{1,0:T(8,128)}, bf16[768,2048]{1,0:T(8,128)(2,1)}, bf16[16,64,768]{2,1,0:T(8,128)(2,1)}, bf16[4,576,768]{2,1,0:T(8,128)(2,1)}) custom-call(bf16[1024,768]{1,0:T(8,128)(2,1)} %get-tuple-element.75.h2_ref.x_ref, bf16[1024,768]{1,0:T(8,128)(2,1)} %bitcast.105, bf16[2,4,4,576,256]{4,3,2,1,0:T(8,128)(2,1)} %bitcast.98, ...), custom_call_target="tpu_custom_call" | custom-call | flops 28991029248 | bytes 25165824 | tf_op jit(solution)/shard_map/shared/pallas_call | solution.py:753
  257.0 27.5 %combine.1 = (bf16[1024,768]{1,0:T(8,128)(2,1)}, f32[1024,768]{1,0:T(8,128)}, bf16[1024,768]{1,0:T(8,128)(2,1)}, bf16[1024,768]{1,0:T(8,128)(2,1)}, f32[8,768]{1...) custom-call(f32[1024,768]{1,0:T(8,128)} %get-tuple-element.74.mid_ref, ...), custom_call_target="tpu_custom_call" | custom-call | flops 11000000512 | bytes 30000000 | tf_op jit(solution)/shard_map/combine/pallas_call | solution.py:875
  284.6 0.0 copy-start.27
  284.6 0.0 copy-start.21
  284.6 0.0 copy-start.24
  284.6 0.0 copy-start.18
  284.7 0.0 copy-start.19
  284.7 90.8 %attention_backward.1 = (f32[1024,768]{1,0:T(8,128)}, f32[4,48,768]{2,1,0:T(8,128)}, f32[2,48,2048]{2,1,0:T(8,128)}, f32[2,64,768]{2,1,0:T(8,128)}, f32[8,768]{1,0:T(8,128)}) custom-call(bf16[3,1024,768]{2,1,0:T(8,128)(2,1)} %get-tuple-element.92.qkv_ref, bf16[1024,768]{1,0:T(8,128)(2,1)} %get-tuple-element.93.og_ref, ...), custom_call_target="tpu_custom_call" | custom-call | flops 80000000000 | bytes 30000000 | tf_op jit(solution)/shard_map/attention_backward/pallas_call | solution.py:1207
  375.5 0.0 copy-start.15
  375.5 0.9 constant_dynamic-slice_fusion
  376.4 0.6 multiply_subtract_fusion.5
  377.0 0.6 multiply_subtract_fusion.4
  377.7 1.7 multiply_subtract_fusion.3
  379.4 0.9 collective-permute-start
  380.4 2.5 multiply_subtract_fusion.2
  382.8 1.3 multiply_subtract_fusion.1
  384.1 1.8 multiply_subtract_fusion
  385.9 1.0 copy-done.1
  387.0 11.0 %adam_blocks.2 = (f32[2,192,2048]{2,1,0:T(8,128)}, f32[2,192,2048]{2,1,0:T(8,128)}, f32[2,192,2048]{2,1,0:T(8,128)}) custom-call(s32[1]{0:T(128)} %bitcast.28.core_ref, f32[2,192,2048]{2,1,0:T(8,128)} %bitcast.73, f32[2,192,2048]{2,1,0:T(8,128)} %bitcast.81, f32[2,192,2048]{2,1,0:T(8,128)} %bitcast.82, bf16[2304,256]{1,0:T(8,128)(2,1)} %bitcast.75, ...), custom_call_target="tpu_custom_call" | custom-call | flops 15728640 | bytes 20447232 | tf_op jit(solution)/shard_map/adam_blocks/pallas_call | solution.py:1295
  398.0 5.1 %adam_blocks.3 = (f32[512,768]{1,0:T(8,128)}, f32[512,768]{1,0:T(8,128)}, f32[512,768]{1,0:T(8,128)}) custom-call(s32[1]{0:T(128)} %bitcast.28.core_ref, f32[512,768]{1,0:T(8,128)} %bitcast.71, f32[512,768]{1,0:T(8,128)} %bitcast.84, f32[512,768]{1,0:T(8,128)} %bitcast.85, bf16[2304,256]{1,0:T(8,128)(2,1)} %bitcast.76, bf16[2304,256]{1,0:T(8,128)(2,1)} %copy-done.1), custom_call_target="tpu_custom_call" | custom-call | flops 7864320 | bytes 10223616 | tf_op jit(solution)/shard_map/adam_blocks/pallas_call | solution.py:1295
  403.1 1.1 copy.77
  404.2 1.3 copy-done.2
  405.5 1.7 copy.78
  (68 shorter events, 0.4 us)
Async XLA Ops:
  7.2 111.5 %all-gather.7.cloned.1.call-start = ((), (), s32[]{:S(2)}) async-start(), calls=%async_computation.3 | async-start | bytes 10616832 | tf_op jit(solution)/shard_map/all_gather | solution.py:1348
  7.3 2.0 copy-start
  9.6 1.4 copy-start.20
  9.6 1.4 copy-start.26
  9.8 2.5 copy-start.6
  10.9 1.5 copy-start.3
  10.9 2.2 copy-start.22
  10.9 3.5 copy-start.13
  10.9 4.2 %copy-start.23 = (s32[1,1024]{1,0:T(1,128)S(1)}, s32[1,1024]{1,0:T(1,128)}, u32[]{:S(2)}) copy-start(s32[1,1024]{1,0:T(1,128)} %param.30) | copy-start | bytes 12292
  10.9 198.0 %all-gather.5.cloned.1.call-start = ((), (), s32[]{:S(2)}) async-start(), calls=%async_computation.2 | async-start | bytes 10616832 | tf_op jit(solution)/shard_map/all_gather | solution.py:1348
  62.2 317.2 %reduce-scatter.2.cloned.1.call-start = ((), (), s32[]{:S(2)}) async-start(), calls=%async_computation.1 | async-start | bytes 5898240 | tf_op jit(solution)/shard_map/reduce_scatter | solution.py:1375
  284.6 91.9 %copy-start.27 = (f32[2,48]{1,0:T(2,128)S(1)}, f32[2,48]{1,0:T(2,128)}, u32[]{:S(2)}) copy-start(f32[2,48]{1,0:T(2,128)} %param.32) | copy-start | bytes 1156
  284.6 91.9 %copy-start.28 = (f32[2,48]{1,0:T(2,128)S(1)}, f32[2,48]{1,0:T(2,128)}, u32[]{:S(2)}) copy-start(f32[2,48]{1,0:T(2,128)} %param.33) | copy-start | bytes 1156
  284.6 91.9 %copy-start.29 = (f32[2,48]{1,0:T(2,128)S(1)}, f32[2,48]{1,0:T(2,128)}, u32[]{:S(2)}) copy-start(f32[2,48]{1,0:T(2,128)} %param.34) | copy-start | bytes 1156
  284.6 92.5 %copy-start.21 = (f32[48,4]{0,1:T(4,128)S(1)}, f32[48,4]{0,1:T(4,128)}, u32[]{:S(2)}) copy-start(f32[48,4]{0,1:T(4,128)} %param.41) | copy-start | bytes 2308
  284.6 92.4 %copy-start.24 = (f32[48,4]{0,1:T(4,128)S(1)}, f32[48,4]{0,1:T(4,128)}, u32[]{:S(2)}) copy-start(f32[48,4]{0,1:T(4,128)} %param.42) | copy-start | bytes 2308
  284.6 92.4 %copy-start.25 = (f32[48,4]{0,1:T(4,128)S(1)}, f32[48,4]{0,1:T(4,128)}, u32[]{:S(2)}) copy-start(f32[48,4]{0,1:T(4,128)} %param.43) | copy-start | bytes 2308
  284.6 93.0 %copy-start.14 = (f32[48,768]{1,0:T(8,128)S(1)}, f32[48,768]{1,0:T(8,128)}, u32[]{:S(2)}) copy-start(f32[48,768]{1,0:T(8,128)} %param.38) | copy-start | bytes 442372
  284.6 93.0 %copy-start.18 = (f32[48,768]{1,0:T(8,128)S(1)}, f32[48,768]{1,0:T(8,128)}, u32[]{:S(2)}) copy-start(f32[48,768]{1,0:T(8,128)} %param.39) | copy-start | bytes 442372
  284.7 93.0 %copy-start.19 = (f32[48,768]{1,0:T(8,128)S(1)}, f32[48,768]{1,0:T(8,128)}, u32[]{:S(2)}) copy-start(f32[48,768]{1,0:T(8,128)} %param.40) | copy-start | bytes 442372
  284.7 95.7 %copy-start.7 = (f32[128,768]{1,0:T(8,128)S(1)}, f32[128,768]{1,0:T(8,128)}, u32[]{:S(2)}) copy-start(f32[128,768]{1,0:T(8,128)} %param.47) | copy-start | bytes 1179652
  284.7 95.7 %copy-start.17 = (f32[128,768]{1,0:T(8,128)S(1)}, f32[128,768]{1,0:T(8,128)}, u32[]{:S(2)}) copy-start(f32[128,768]{1,0:T(8,128)} %param.48) | copy-start | bytes 1179652
  375.5 7.3 %copy-start.4 = (f32[3,48,768]{2,1,0:T(8,128)S(1)}, f32[3,48,768]{2,1,0:T(8,128)}, u32[]{:S(2)}) copy-start(f32[3,48,768]{2,1,0:T(8,128)} %param.35) | copy-start | bytes 1327108
  375.5 7.3 %copy-start.12 = (f32[4,48,768]{2,1,0:T(8,128)S(1)}, f32[4,48,768]{2,1,0:T(8,128)}, u32[]{:S(2)}) copy-start(f32[4,48,768]{2,1,0:T(8,128)} %get-tuple-element.104) | copy-start | bytes 1769476
  375.5 7.3 %copy-start.15 = (f32[3,48,768]{2,1,0:T(8,128)S(1)}, f32[3,48,768]{2,1,0:T(8,128)}, u32[]{:S(2)}) copy-start(f32[3,48,768]{2,1,0:T(8,128)} %param.36) | copy-start | bytes 1327108
  375.5 7.3 %copy-start.16 = (f32[3,48,768]{2,1,0:T(8,128)S(1)}, f32[3,48,768]{2,1,0:T(8,128)}, u32[]{:S(2)}) copy-start(f32[3,48,768]{2,1,0:T(8,128)} %param.37) | copy-start | bytes 1327108
  379.4 6.5 %collective-permute-start = (bf16[2304,256]{1,0:T(8,128)(2,1)}, bf16[2304,256]{1,0:T(8,128)(2,1)S(1)}, u32[]{:S(2)}, u32[]{:S(2)}) collective-permute-start(bf16[2304,256]{1,0:T(8,128)(2,1)} %bitcast.74), channel_id=1, source_target_pairs={{0,16},{16,0},{1,17},{17,1},{2,18},{18,2},{3,19},{19,3},{4,20},{20... | collective-permute-start | bytes 3538952 | tf_op jit(solution)/shard_map/ppermute | solution.py:1319
  380.3 3.8 copy-start.8
  380.3 3.8 copy-start.9
  380.3 3.8 copy-start.10
  380.4 3.8 copy-start.11
  385.9 1.0 copy-start.1
  398.0 5.1 %copy-start.5 = (bf16[1024,768]{1,0:T(8,128)(2,1)S(1)}, bf16[1024,768]{1,0:T(8,128)(2,1)}, u32[]{:S(2)}) copy-start(bf16[1024,768]{1,0:T(8,128)(2,1)} %get-tuple-element.91) | copy-start | bytes 4718596
  403.1 2.5 copy-start.2
Sparse Core Ops, SparseCore 0:
  11.0 104.8 all-gather.6
  117.5 90.4 all-gather.4
  210.3 88.6 reduce-scatter.1
